TPU v7x, 128 devices: a whole 4x4x4 slice. The times are simulated.
128 devices in a mesh: grp: 4 (over z_lo, core), lon: 32 (over x, y, z_hi).
Axes of the slice: x: 4, y: 4, z: 4 (z_hi: 2, z_lo: 2; z = z_hi * 2 + z_lo), core: 2. Of those that a mesh axis runs over, the one named last changes fastest.
Arguments:
- field: float32 [16, 1024, 128], P('grp', 'lon'), may hold values from -6 to 6
- wind: float32 [16, 1024, 128], P('grp', 'lon'), may hold values from -1 to 1
- w_in: bfloat16 [128, 2048], replicated, may hold values from -0.5 to 0.5
- w_mid: bfloat16 [2048, 2048], replicated, may hold values from -0.125 to 0.125
- w_out: bfloat16 [2048, 128], replicated, may hold values from -0.125 to 0.125
- targets: float32 [4096, 128], P('lon'), may hold values from -6 to 6
- column_map: int32 [4, 32, 128, 1], P('grp', 'lon'), may hold values from 0 to 31; in each aligned block of 128 rows (0 to 127, 128 to 255, ..., all dimensions but the last counted through in order) at most 8 rows name the same one
- batch_count: int32 [32], replicated, may hold values from 1 to 128, 2048 in all
Outputs:
- field_out: float32 [16, 1024, 128], P('grp', 'lon')
- grad_mid: float32 [2048, 2048], P(('grp', 'lon'))
- grad_out: float32 [2048, 128], P(('grp', 'lon'))
Inputs may be any that keep to these rules, and one draw needn't show every extreme that they name: `column_map`: among the 128 columns of one device in the first 3 bands at most 8 name one trainer, and that bound is reached. The last band's entries are not read. `batch_count`: the largest entry equals 128.
All inputs are finite; a program needn't handle non-finite values.
Results may differ from a plain program's by a relative error of at most 0.0034.
Values may be sent and summed in bfloat16 or wider, within the bound.
A program may use at most 128 MiB of HBM per device.

v0:
```python
import jax
import jax.numpy as jnp
from jax import lax
from jax.sharding import PartitionSpec as P

STEPS = 2


loss_scale = 1024.0
physics_share = 0.5


def padded_2(cells, sides, width):
    for axis, dim in sides:
        count = lax.axis_size(axis)
        head = lax.slice_in_dim(cells, 0, width, axis=dim)
        tail = lax.slice_in_dim(cells, cells.shape[dim] - width, cells.shape[dim], axis=dim)
        cells = jnp.concatenate(
            [
                lax.ppermute(tail, axis, [(i, (i + 1) % count) for i in range(count)]),
                cells,
                lax.ppermute(head, axis, [((i + 1) % count, i) for i in range(count)]),
            ],
            axis=dim,
        )
    return cells


def silu_slope(values):
    sig = jax.nn.sigmoid(values)
    return sig * (1.0 + values * (1.0 - sig))


def network_pass(inputs, wanted, weights, w_in, w_mid, w_out):
    first_pre = jnp.dot(inputs, w_in, preferred_element_type=jnp.float32)
    first_act = jax.nn.silu(first_pre).astype(jnp.bfloat16)
    second_pre = jnp.dot(first_act, w_mid, preferred_element_type=jnp.float32)
    second_act = jax.nn.silu(second_pre).astype(jnp.bfloat16)
    predicted = jnp.dot(second_act, w_out, preferred_element_type=jnp.float32)
    out_slope = ((predicted - wanted) * weights[:, None]).astype(jnp.bfloat16)
    back_hidden = lax.dot_general(
        out_slope, w_out, (((1,), (1,)), ((), ())), preferred_element_type=jnp.float32
    )
    mid_slope = (back_hidden * silu_slope(second_pre)).astype(jnp.bfloat16)
    return (predicted, first_act, second_act, out_slope, mid_slope)


def stencil(padded, wind_band):
    center = padded[1:-1, 1:-1]
    eastern = padded[1:-1, 2:]
    western = padded[1:-1, :-2]
    northern = padded[2:, 1:-1]
    southern = padded[:-2, 1:-1]
    return (
        center
        - 0.25 * wind_band * (eastern - western)
        + 0.15 * (eastern + western + northern + southern - 4.0 * center)
    )


def body(field, wind, w_in, w_mid, w_out, targets, column_map, batch_count):
    group_index = lax.axis_index("grp")
    lon_index = lax.axis_index("lon")
    n_grp = lax.axis_size("grp")
    n_lon = lax.axis_size("lon")
    lat_rows, lon_cells, levels = field.shape
    columns = lat_rows * lon_cells
    capacity = max(2, 2 * columns // n_lon)
    hidden = w_mid.shape[0]
    slot_rows = (n_grp - 1) * n_lon * capacity
    is_trainer = group_index == n_grp - 1
    low_edge = group_index == 0
    high_edge = group_index == n_grp - 2
    current = field
    for iteration in range(STEPS):
        padded = padded_2(current, (("grp", 0), ("lon", 1)), 1)
        row_ids = jnp.arange(padded.shape[0])
        outside = (row_ids < 1) & low_edge | (row_ids >= padded.shape[0] - 1) & high_edge
        current = stencil(jnp.where(outside[:, None, None], 0.0, padded), wind)
    trainer_of = column_map.reshape(columns)
    matches = (trainer_of[:, None] == jnp.arange(n_lon)[None, :]).astype(jnp.int32)
    position = jnp.sum((jnp.cumsum(matches, 0) - matches) * matches, 1)
    slots = trainer_of * capacity + position
    start_rows = field.reshape(columns, levels).astype(jnp.bfloat16)
    increment = (current - field).reshape(columns, levels).astype(jnp.bfloat16)
    payload = jnp.concatenate([start_rows, increment], 1)
    packed = jnp.zeros((n_lon * capacity, 2 * levels), jnp.bfloat16).at[slots].set(payload)
    flags = jnp.zeros((n_lon * capacity,), jnp.bfloat16).at[slots].set(1.0)
    outgoing = (
        jnp.zeros((n_grp, n_lon, capacity, 2 * levels), jnp.bfloat16)
        .at[n_grp - 1]
        .set(packed.reshape(n_lon, capacity, 2 * levels))
    )
    out_flags = (
        jnp.zeros((n_grp, n_lon, capacity), jnp.bfloat16)
        .at[n_grp - 1]
        .set(flags.reshape(n_lon, capacity))
    )
    incoming, arrived = (
        lax.all_to_all(
            lax.all_to_all(outgoing, "grp", split_axis=0, concat_axis=0, tiled=True),
            "lon",
            split_axis=1,
            concat_axis=1,
            tiled=True,
        ),
        lax.all_to_all(
            lax.all_to_all(out_flags, "grp", split_axis=0, concat_axis=0, tiled=True),
            "lon",
            split_axis=1,
            concat_axis=1,
            tiled=True,
        ),
    )
    replay = field.reshape(columns, levels).astype(jnp.bfloat16)

    def train_branch(operands):
        received, received_flags = operands
        arrived_rows = received[: n_grp - 1].reshape(slot_rows, 2 * levels)
        filled_rows = received_flags[: n_grp - 1].reshape(slot_rows).astype(jnp.float32)
        inputs = jnp.concatenate([arrived_rows[:, :levels], replay], 0)
        wanted = jnp.concatenate([arrived_rows[:, levels:].astype(jnp.float32), targets], 0)
        batch_rows = lax.dynamic_index_in_dim(batch_count, lon_index, 0, keepdims=False)
        in_batch = (jnp.arange(columns) < batch_rows).astype(jnp.float32)
        row_total = batch_rows.astype(jnp.float32) + jnp.sum(filled_rows)
        loss_weight = loss_scale / (n_lon * row_total)
        weights = jnp.concatenate([filled_rows, in_batch], 0) * loss_weight
        predicted, first_act, second_act, out_slope, mid_slope = network_pass(
            inputs, wanted, weights, w_in, w_mid, w_out
        )
        tendency = (
            predicted[:slot_rows].astype(jnp.bfloat16).reshape(n_grp - 1, n_lon, capacity, levels)
        )
        tendency = jnp.concatenate(
            [tendency, jnp.zeros((1, n_lon, capacity, levels), jnp.bfloat16)], 0
        )
        return (tendency, predicted[slot_rows:], first_act, second_act, out_slope, mid_slope)

    def resting_branch(operands):
        total_rows = slot_rows + columns
        return (
            jnp.zeros((n_grp, n_lon, capacity, levels), jnp.bfloat16),
            jnp.zeros((columns, levels), jnp.float32),
            jnp.zeros((total_rows, hidden), jnp.bfloat16),
            jnp.zeros((total_rows, hidden), jnp.bfloat16),
            jnp.zeros((total_rows, levels), jnp.bfloat16),
            jnp.zeros((total_rows, hidden), jnp.bfloat16),
        )

    tendency, replay_pred, first_act, second_act, out_slope, mid_slope = lax.cond(
        is_trainer, train_branch, resting_branch, (incoming, arrived)
    )
    returned = lax.all_to_all(
        lax.all_to_all(tendency, "grp", split_axis=0, concat_axis=0, tiled=True),
        "lon",
        split_axis=1,
        concat_axis=1,
        tiled=True,
    )
    column_tendency = returned[n_grp - 1].reshape(n_lon * capacity, levels)[slots]
    column_tendency = lax.optimization_barrier(column_tendency).astype(jnp.float32)
    sim_out = current + physics_share * column_tendency.reshape(lat_rows, lon_cells, levels)
    field_out = jnp.where(is_trainer, replay_pred.reshape(lat_rows, lon_cells, levels), sim_out)
    part_mid = lax.dot_general(
        first_act, mid_slope, (((0,), (0,)), ((), ())), preferred_element_type=jnp.float32
    )
    part_out = lax.dot_general(
        second_act, out_slope, (((0,), (0,)), ((), ())), preferred_element_type=jnp.float32
    )
    summed = lax.psum_scatter(
        jnp.concatenate([part_mid, part_out], 1), ("grp", "lon"), scatter_dimension=0, tiled=True
    )
    return (field_out, summed[:, :hidden], summed[:, hidden:])


def solution(mesh):
    placed = (
        P("grp", "lon", None),
        P("grp", "lon", None),
        P(),
        P(),
        P(),
        P("lon", None),
        P("grp", "lon", None, None),
        P(),
    )
    return jax.shard_map(
        body,
        mesh=mesh,
        in_specs=placed,
        out_specs=(P("grp", "lon", None), P(("grp", "lon"), None), P(("grp", "lon"), None)),
        check_vma=False,
    )
```

profile of v0, /device:TPU:1, one launch (start us, length us, event | category | flops | bytes accessed | tf_op | source)
XLA Modules:
  0.0 867.2 jit_solution(10660818240158047992)
XLA Ops:
  7.2 0.7 fusion.25
  7.9 1.4 collective-permute-start.1
  9.3 1.6 collective-permute-start
  10.9 0.7 fusion.17
  11.8 0.8 select_reduce_fusion
  12.7 0.8 constant_dynamic-update-slice_fusion.1
  13.6 3.4 collective-permute-start.2
  17.0 4.7 collective-permute-start.3
  21.7 0.9 collective-permute-done.2
  22.7 0.9 fusion.12
  23.6 2.0 collective-permute-start.4
  25.6 0.2 collective-permute-start.5
  25.8 0.7 fusion.19
  26.5 1.3 scatter_custom_fusion.1
  28.0 0.7 collective-permute-done.5
  28.7 1.5 collective-permute-start.6
  30.3 6.6 collective-permute-start.7
  36.9 0.7 reshape.191
  37.6 4.0 all-to-all-start.2
  41.6 1.0 subtract_convert_fusion
  42.6 1.1 scatter_custom_fusion
  43.7 0.8 scatter.25
  44.5 4.1 all-to-all-start
  48.7 0.7 copy.29
  49.4 7.2 all-to-all-done
  56.6 6.1 all-to-all-start.3
  62.8 0.9 copy.27
  63.6 7.7 all-to-all-done.3
  71.4 3.9 all-to-all-start.1
  75.3 11.3 %all-to-all-done.1 = bf16[4,32,8,256]{3,2,0,1:T(8,128)(2,1)S(1)} async-done(((bf16[4,32,8,256]{3,2,0,1:T(8,128)(2,1)}), bf16[4,32,8,256]{3,2,0,1:T(8,128)(2,1)S(1)}, u32[]{:S(2)}, u32[]{:S(2)}) %all-to-all-start.1) | async-done | bytes 524320 | tf_op jit(solution)/shard_map/all_to_all | solution.py:100
  86.6 7.7 conditional.1
  86.6 0.7 broadcast.121
  87.4 2.4 broadcast.120.clone.1
  89.8 2.3 broadcast.120.clone
  92.1 2.2 broadcast.120
  94.3 2.8 fusion.27
  97.1 12.9 %fusion.26 = f32[2048,2048]{0,1:T(8,128)S(1)} fusion(bf16[896,2048]{1,0:T(8,128)(2,1)} %get-tuple-element.63, bf16[896,2048]{1,0:T(8,128)(2,1)} %get-tuple-element.64), kind=kOutput, calls=%fused_computation.62 | convolution fusion | flops 7516192768 | bytes 24117248 | tf_op jit(solution)/shard_map/dot_general | solution.py:164
  110.0 7.6 pad_maximum_fusion
  117.7 18.0 %copy.35 = f32[2048,2176]{1,0:T(8,128)} copy(f32[2048,2176]{0,1:T(8,128)} %pad_maximum_fusion) | data formatting | bytes 35651584
  135.7 32.2 %all_to_all.30 = bf16[4,32,8,128]{3,2,1,0:T(8,128)(2,1)S(1)} all-to-all(bf16[4,32,8,128]{3,2,1,0:T(8,128)(2,1)S(1)} %get-tuple-element.62), channel_id=1, replica_groups=mesh['grp'=4,'lon'=32] {'grp'}, dimensions={0} | all-to-all | bytes 524288 | tf_op jit(solution)/shard_map/all_to_all | solution.py:154
  167.9 0.8 copy.32
  168.6 3.9 all-to-all-start.5
  172.5 10.1 %all-to-all-done.5 = bf16[4,32,8,128]{3,2,0,1:T(8,128)(2,1)S(1)} async-done(((bf16[4,32,8,128]{3,2,0,1:T(8,128)(2,1)}), bf16[4,32,8,128]{3,2,0,1:T(8,128)(2,1)S(1)}, u32[]{:S(2)}, u32[]{:S(2)}) %all-to-all-start.5) | async-done | bytes 262176 | tf_op jit(solution)/shard_map/all_to_all | solution.py:153
  182.6 0.7 gather_fusion
  183.3 0.6 add_select_fusion
  184.0 673.5 %reduce-scatter.4.cloned.1.call-done = f32[16,2176]{1,0:T(8,128)} async-done(((f32[2048,2176]{1,0:T(8,128)}), f32[16,2176]{1,0:T(8,128)}) %reduce-scatter.4.cloned.1.call-update) | async-done | bytes 139280
  857.5 1.3 slice.170
  858.8 1.6 slice.169
  (28 shorter events, 0.8 us)
Async XLA Ops:
  7.9 5.7 collective-permute-start.1
  9.3 3.4 collective-permute-start
  13.6 9.0 %collective-permute-start.2 = (f32[6,1,128]{2,1,0:T(1,128)S(1)}, f32[6,1,128]{2,1,0:T(1,128)S(1)}, u32[]{:S(2)}, u32[]{:S(2)}) collective-permute-start(f32[6,1,128]{2,1,0:T(1,128)S(1)} %get-tuple-element.117), channel_id=1, source_target_pairs={{0,1},{1,2},{2,3},{3,4},{4,5},{5,6},{6,7},{7,8},{8,9},{9,10},{10,1... | collective-permute-start | bytes 9224 | tf_op jit(solution)/shard_map/ppermute | solution.py:20
  17.0 5.6 collective-permute-start.3
  23.6 4.4 collective-permute-start.4
  25.6 3.2 collective-permute-start.5
  28.7 12.8 %collective-permute-start.6 = (f32[6,1,128]{2,1,0:T(1,128)S(1)}, f32[6,1,128]{2,1,0:T(1,128)S(1)}, u32[]{:S(2)}, u32[]{:S(2)}) collective-permute-start(f32[6,1,128]{2,1,0:T(1,128)S(1)} %get-tuple-element.115), channel_id=1, source_target_pairs={{0,1},{1,2},{2,3},{3,4},{4,5},{5,6},{6,7},{7,8},{8,9},{9,10},{10,1... | collective-permute-start | bytes 9224 | tf_op jit(solution)/shard_map/ppermute | solution.py:20
  30.3 11.2 %collective-permute-start.7 = (f32[6,1,128]{2,1,0:T(1,128)S(1)}, f32[6,1,128]{2,1,0:T(1,128)S(1)}, u32[]{:S(2)}, u32[]{:S(2)}) collective-permute-start(f32[6,1,128]{2,1,0:T(1,128)S(1)} %get-tuple-element.116), channel_id=1, source_target_pairs={{1,0},{2,1},{3,2},{4,3},{5,4},{6,5},{7,6},{8,7},{9,8},{10,9},{11,1... | collective-permute-start | bytes 9224 | tf_op jit(solution)/shard_map/ppermute | solution.py:22
  37.6 6.9 all-to-all-start.2
  44.5 12.1 %all-to-all-start = ((bf16[4,32,8,256]{3,2,1,0:T(8,128)(2,1)}), bf16[4,32,8,256]{3,2,1,0:T(8,128)(2,1)S(1)}, u32[]{:S(2)}, u32[]{:S(2)}) async-start(bf16[4,32,8,256]{3,2,1,0:T(8,128)(2,1)} %scatter.25), calls=%async_computation | async-start | bytes 1048576 | tf_op jit(solution)/shard_map/all_to_all | solution.py:101
  56.6 14.8 %all-to-all-start.3 = ((bf16[4,32,8]{2,0,1:T(4,128)(2,1)}), bf16[4,32,8]{2,0,1:T(4,128)(2,1)S(1)}, u32[]{:S(2)}, u32[]{:S(2)}) async-start(bf16[4,32,8]{2,0,1:T(4,128)(2,1)} %copy.29), calls=%async_computation.3 | async-start | bytes 65536 | tf_op jit(solution)/shard_map/all_to_all | solution.py:107
  71.4 15.2 %all-to-all-start.1 = ((bf16[4,32,8,256]{3,2,0,1:T(8,128)(2,1)}), bf16[4,32,8,256]{3,2,0,1:T(8,128)(2,1)S(1)}, u32[]{:S(2)}, u32[]{:S(2)}) async-start(bf16[4,32,8,256]{3,2,0,1:T(8,128)(2,1)} %copy.27), calls=%async_computation.1 | async-start | bytes 1048576 | tf_op jit(solution)/shard_map/all_to_all | solution.py:100
  75.3 782.2 %reduce-scatter.4.cloned.1.call-start = ((), (), s32[]{:S(2)}) async-start(), calls=%async_computation.7 | async-start | bytes 17965056
  168.6 14.0 %all-to-all-start.5 = ((bf16[4,32,8,128]{3,2,0,1:T(8,128)(2,1)}), bf16[4,32,8,128]{3,2,0,1:T(8,128)(2,1)S(1)}, u32[]{:S(2)}, u32[]{:S(2)}) async-start(bf16[4,32,8,128]{3,2,0,1:T(8,128)(2,1)} %copy.32), calls=%async_computation.5 | async-start | bytes 524288 | tf_op jit(solution)/shard_map/all_to_all | solution.py:153
Sparse Core Ops, SparseCore 0:
  135.8 721.6 reduce-scatter.3
where the time goes:
time: 868 us; the launch traced here: 867 us
  waiting for transfers between devices  711 us (82%)
  starting transfers between devices  43.5 us (5%)
  local copies, waits for them, and re-layouts  36.3 us (4%)
  blocking collectives  32.2 us (4%)
  matrix products  15.7 us (2%)
  between operations  14.2 us (2%)
  other arithmetic  13.8 us (2%)
    unnamed x2, waiting for transfers between devices  673 us
    all_to_all x1, blocking collectives, body(): lax.all_to_all(tendency, 'grp', split_axis=0, concat_axis=0, tiled=True)  32.2 us
    unnamed x7, local copies, waits for them, and re-layouts  19.7 us
  transfers between devices with their start and end apart: 14, of which 7 were waited for; matrix products, arithmetic and copies ran while one was open for 1% of the time, Pallas kernels for 0%

commit v1 on v0

v1 whole, which is shorter than its diff:
```python
import jax
import jax.numpy as jnp
from jax import lax
from jax.sharding import PartitionSpec as P

STEPS = 2


loss_scale = 1024.0
physics_share = 0.5


def padded_2(cells, sides, width):
    for axis, dim in sides:
        count = lax.axis_size(axis)
        head = lax.slice_in_dim(cells, 0, width, axis=dim)
        tail = lax.slice_in_dim(cells, cells.shape[dim] - width, cells.shape[dim], axis=dim)
        cells = jnp.concatenate(
            [
                lax.ppermute(tail, axis, [(i, (i + 1) % count) for i in range(count)]),
                cells,
                lax.ppermute(head, axis, [((i + 1) % count, i) for i in range(count)]),
            ],
            axis=dim,
        )
    return cells


def silu_slope(values):
    sig = jax.nn.sigmoid(values)
    return sig * (1.0 + values * (1.0 - sig))


def network_pass(inputs, wanted, weights, w_in, w_mid, w_out):
    first_pre = jnp.dot(inputs, w_in, preferred_element_type=jnp.float32)
    first_act = jax.nn.silu(first_pre).astype(jnp.bfloat16)
    second_pre = jnp.dot(first_act, w_mid, preferred_element_type=jnp.float32)
    second_act = jax.nn.silu(second_pre).astype(jnp.bfloat16)
    predicted = jnp.dot(second_act, w_out, preferred_element_type=jnp.float32)
    out_slope = ((predicted - wanted) * weights[:, None]).astype(jnp.bfloat16)
    back_hidden = lax.dot_general(
        out_slope, w_out, (((1,), (1,)), ((), ())), preferred_element_type=jnp.float32
    )
    mid_slope = (back_hidden * silu_slope(second_pre)).astype(jnp.bfloat16)
    return (predicted, first_act, second_act, out_slope, mid_slope)


def stencil(padded, wind_band):
    center = padded[1:-1, 1:-1]
    eastern = padded[1:-1, 2:]
    western = padded[1:-1, :-2]
    northern = padded[2:, 1:-1]
    southern = padded[:-2, 1:-1]
    return (
        center
        - 0.25 * wind_band * (eastern - western)
        + 0.15 * (eastern + western + northern + southern - 4.0 * center)
    )


def body(field, wind, w_in, w_mid, w_out, targets, column_map, batch_count):
    group_index = lax.axis_index("grp")
    lon_index = lax.axis_index("lon")
    n_grp = lax.axis_size("grp")
    n_lon = lax.axis_size("lon")
    lat_rows, lon_cells, levels = field.shape
    columns = lat_rows * lon_cells
    hidden = w_mid.shape[0]
    is_trainer = group_index == n_grp - 1
    low_edge = group_index == 0
    high_edge = group_index == n_grp - 2
    current = field
    for iteration in range(STEPS):
        padded = padded_2(current, (("grp", 0), ("lon", 1)), 1)
        row_ids = jnp.arange(padded.shape[0])
        outside = (row_ids < 1) & low_edge | (row_ids >= padded.shape[0] - 1) & high_edge
        current = stencil(jnp.where(outside[:, None, None], 0.0, padded), wind)
    trainer_of = column_map.reshape(columns)
    matches = (trainer_of[:, None] == jnp.arange(n_lon)[None, :]).astype(jnp.float32)
    loads = lax.psum(jnp.where(is_trainer, 0.0, jnp.sum(matches, 0)), ("grp", "lon"))
    trainer_weight = loss_scale / (n_lon * (batch_count.astype(jnp.float32) + loads))
    column_weight = jnp.sum(matches * trainer_weight[None, :], 1)
    batch_rows = lax.dynamic_index_in_dim(batch_count, lon_index, 0, keepdims=False)
    own_weight = lax.dynamic_index_in_dim(trainer_weight, lon_index, 0, keepdims=False)
    replay_weight = jnp.where(jnp.arange(columns) < batch_rows, own_weight, 0.0)
    weights = jnp.where(is_trainer, replay_weight, column_weight)
    inputs = field.reshape(columns, levels).astype(jnp.bfloat16)
    increment = (current - field).reshape(columns, levels).astype(jnp.bfloat16)
    wanted = jnp.where(is_trainer, targets, increment.astype(jnp.float32))
    predicted, first_act, second_act, out_slope, mid_slope = network_pass(
        inputs, wanted, weights, w_in, w_mid, w_out
    )
    tendency = lax.reduce_precision(predicted, 8, 7)
    sim_out = current + physics_share * tendency.reshape(lat_rows, lon_cells, levels)
    field_out = jnp.where(is_trainer, predicted.reshape(lat_rows, lon_cells, levels), sim_out)
    part_mid = lax.dot_general(
        first_act, mid_slope, (((0,), (0,)), ((), ())), preferred_element_type=jnp.float32
    )
    part_out = lax.dot_general(
        second_act, out_slope, (((0,), (0,)), ((), ())), preferred_element_type=jnp.float32
    )
    summed = lax.psum_scatter(
        jnp.concatenate([part_mid, part_out], 1), ("grp", "lon"), scatter_dimension=0, tiled=True
    )
    return (field_out, summed[:, :hidden], summed[:, hidden:])


def solution(mesh):
    placed = (
        P("grp", "lon", None),
        P("grp", "lon", None),
        P(),
        P(),
        P(),
        P("lon", None),
        P("grp", "lon", None, None),
        P(),
    )
    return jax.shard_map(
        body,
        mesh=mesh,
        in_specs=placed,
        out_specs=(P("grp", "lon", None), P(("grp", "lon"), None), P(("grp", "lon"), None)),
        check_vma=False,
    )
```

time: 868 us -> 870 us (level)
  blocking collectives: 32.2 us -> 67.4 us
  starting transfers between devices: 43.5 us -> 20.7 us
  local copies, waits for them, and re-layouts: 36.3 us -> 24.4 us
    psum x0 -> x1, blocking collectives: none -> 67.4 us  [body(): lax.psum(jnp.where(is_trainer, 0.0, jnp.sum(matches, 0)), ('grp', 'lon'))]
    all_to_all x5 -> x0, waiting for transfers between devices: 36.3 us -> none  [the longest x1 11.3 us: body(): lax.all_to_all(lax.all_to_all(outgoing, 'grp', split_axis=0, concat_axis=...]
    unnamed x2, waiting for transfers between devices: 673 us -> 707 us
    all_to_all x1 -> x0, blocking collectives: 32.2 us -> none  [body(): lax.all_to_all(tendency, 'grp', split_axis=0, concat_axis=0, tiled=True)]
    all_to_all x5 -> x0, starting transfers between devices: 22 us -> none  [the longest x1 6.13 us: body(): lax.all_to_all(lax.all_to_all(out_flags, 'grp', split_axis=0, concat_axis...]
  transfers between devices with their start and end apart: 14 -> 9, of which waited for: 7 -> 3; matrix products, arithmetic and copies ran while one was open for 1% -> 1% of each run, Pallas kernels for 0% -> 0%
where the time goes in v1:
time: 870 us; the launch traced here: 869 us
  waiting for transfers between devices  708 us (81%)
  blocking collectives  67.4 us (8%)
  local copies, waits for them, and re-layouts  24.4 us (3%)
  starting transfers between devices  20.7 us (2%)
  other arithmetic  18.1 us (2%)
  matrix products  16.4 us (2%)
  between operations  14.1 us (2%)
    unnamed x2, waiting for transfers between devices  707 us
    psum x1, blocking collectives, body(): lax.psum(jnp.where(is_trainer, 0.0, jnp.sum(matches, 0)), ('grp', 'lon'))  67.4 us
    unnamed x7, local copies, waits for them, and re-layouts  18.9 us
  transfers between devices with their start and end apart: 9, of which 3 were waited for; matrix products, arithmetic and copies ran while one was open for 1% of the time, Pallas kernels for 0%

profile of v1, /device:TPU:1, one launch (start us, length us, event | category | flops | bytes accessed | tf_op | source)
XLA Modules:
  0.0 869.1 jit_solution(10504310171946761518)
XLA Ops:
  7.2 0.0 copy-start
  7.2 0.0 copy-start.1
  7.2 0.0 reduce-scatter.4.cloned.1.call-start
  7.2 0.8 fusion.21
  8.0 1.4 collective-permute-start.1
  9.4 0.8 convert_reduce_fusion
  10.2 1.7 collective-permute-start
  11.9 67.4 %psum.7 = f32[32]{0:T(128)S(1)} all-reduce(f32[32]{0:T(128)S(1)} %broadcast_select_fusion), channel_id=1, replica_groups=mesh['grp'=4,'lon'=32] {'grp','lon'}, use_global_device_ids=true, to_apply=%region_1.2 | all-reduce | flops 32 | bytes 256 | tf_op jit(solution)/shard_map/psum | solution.py:80
  79.3 0.7 multiply_divide_fusion
  79.9 0.0 collective-permute-done
  79.9 0.8 constant_dynamic-update-slice_fusion.1
  80.8 0.0 collective-permute-done.1
  80.8 1.2 collective-permute-start.2
  82.0 6.0 collective-permute-start.3
  88.1 1.0 collective-permute-done.2
  89.0 0.0 collective-permute-done.3
  89.1 0.1 maximum_select_fusion
  89.1 0.9 fusion.12
  90.0 1.6 collective-permute-start.4
  91.6 0.6 collective-permute-start.5
  92.2 0.7 select_reduce_fusion
  92.9 1.2 dynamic_slice.8
  94.2 0.6 dynamic_slice.9
  94.8 0.0 collective-permute-done.4
  94.8 0.1 collective-permute-done.5
  94.9 0.5 collective-permute-start.6
  95.4 7.7 collective-permute-start.7
  103.1 1.3 broadcast_select_fusion.1
  104.4 0.0 collective-permute-done.6
  104.4 0.0 collective-permute-done.7
  104.4 0.1 maximum_select_fusion.1
  104.5 1.0 subtract_convert_fusion
  105.4 1.3 fusion.22
  106.8 5.7 multiply_convert_fusion
  112.5 0.0 copy-done
  112.5 0.0 copy-done.1
  112.5 0.3 fusion.15
  112.8 0.3 fusion.23
  113.1 8.7 fusion.1
  121.8 11.9 %pad_maximum_fusion = f32[2048,2176]{0,1:T(8,128)} fusion(f32[2048,128]{0,1:T(8,128)S(1)} %fusion.23, f32[2048,2048]{0,1:T(8,128)} %fusion.1), kind=kLoop, calls=%fused_computation | loop fusion | flops 4456448 | bytes 35651584 | tf_op jit(solution)/shard_map/concatenate | solution.py:103
  133.7 18.0 %copy.17 = f32[2048,2176]{1,0:T(8,128)} copy(f32[2048,2176]{0,1:T(8,128)} %pad_maximum_fusion) | data formatting | bytes 35651584
  151.8 0.0 reduce-scatter.4.cloned.1.call-update
  151.8 0.6 add_select_fusion
  152.5 706.9 %reduce-scatter.4.cloned.1.call-done = f32[16,2176]{1,0:T(8,128)} async-done(((f32[2048,2176]{1,0:T(8,128)}), f32[16,2176]{1,0:T(8,128)}) %reduce-scatter.4.cloned.1.call-update) | async-done | bytes 139280
  859.4 1.3 slice.95
  860.7 1.6 slice.94
  (7 shorter events, 0.0 us)
Async XLA Ops:
  7.2 105.3 %copy-start = (bf16[2048,128]{1,0:T(8,128)(2,1)S(1)}, bf16[2048,128]{1,0:T(8,128)(2,1)}, u32[]{:S(2)}) copy-start(bf16[2048,128]{1,0:T(8,128)(2,1)} %param.12) | copy-start | bytes 1572868
  7.2 105.3 %copy-start.1 = (f32[128,128]{1,0:T(8,128)S(1)}, f32[128,128]{1,0:T(8,128)}, u32[]{:S(2)}) copy-start(f32[128,128]{1,0:T(8,128)} %param.13) | copy-start | bytes 196612
  7.2 852.2 %reduce-scatter.4.cloned.1.call-start = ((), (), s32[]{:S(2)}) async-start(), calls=%async_computation.1 | async-start | bytes 17965056
  8.0 72.8 %collective-permute-start.1 = (f32[1,32,128]{2,1,0:T(8,128)S(1)}, f32[1,32,128]{2,1,0:T(8,128)S(1)}, u32[]{:S(2)}, u32[]{:S(2)}) collective-permute-start(f32[1,32,128]{2,1,0:T(8,128)S(1)} %get-tuple-element.23), channel_id=1, source_target_pairs={{32,0},{64,32},{96,64},{0,96},{33,1},{65,33},{97,65},{1,97},{34,2}... | collective-permute-start | bytes 49160 | tf_op jit(solution)/shard_map/ppermute | solution.py:22
  10.2 69.7 %collective-permute-start = (f32[1,32,128]{2,1,0:T(8,128)S(1)}, f32[1,32,128]{2,1,0:T(8,128)S(1)}, u32[]{:S(2)}, u32[]{:S(2)}) collective-permute-start(f32[1,32,128]{2,1,0:T(8,128)S(1)} %get-tuple-element.24), channel_id=1, source_target_pairs={{0,32},{32,64},{64,96},{96,0},{1,33},{33,65},{65,97},{97,1},{2,34}... | collective-permute-start | bytes 49160 | tf_op jit(solution)/shard_map/ppermute | solution.py:20
  80.8 8.2 collective-permute-start.2
  82.0 7.0 collective-permute-start.3
  90.0 4.7 collective-permute-start.4
  91.6 3.2 collective-permute-start.5
  94.9 9.5 %collective-permute-start.6 = (f32[6,1,128]{2,1,0:T(1,128)S(1)}, f32[6,1,128]{2,1,0:T(1,128)S(1)}, u32[]{:S(2)}, u32[]{:S(2)}) collective-permute-start(f32[6,1,128]{2,1,0:T(1,128)S(1)} %get-tuple-element.14), channel_id=1, source_target_pairs={{0,1},{1,2},{2,3},{3,4},{4,5},{5,6},{6,7},{7,8},{8,9},{9,10},{10,1... | collective-permute-start | bytes 9224 | tf_op jit(solution)/shard_map/ppermute | solution.py:20
  95.4 9.0 %collective-permute-start.7 = (f32[6,1,128]{2,1,0:T(1,128)S(1)}, f32[6,1,128]{2,1,0:T(1,128)S(1)}, u32[]{:S(2)}, u32[]{:S(2)}) collective-permute-start(f32[6,1,128]{2,1,0:T(1,128)S(1)} %get-tuple-element.15), channel_id=1, source_target_pairs={{1,0},{2,1},{3,2},{4,3},{5,4},{6,5},{7,6},{8,7},{9,8},{10,9},{11,1... | collective-permute-start | bytes 9224 | tf_op jit(solution)/shard_map/ppermute | solution.py:22
Sparse Core Ops, SparseCore 0:
  151.9 707.4 reduce-scatter.3

commit v2 on v1

v2 whole, which is shorter than its diff:
```python
import jax
import jax.numpy as jnp
from jax import lax
from jax.experimental import pallas as pl
from jax.experimental.pallas import tpu as pltpu
from jax.sharding import PartitionSpec as P

MESH = pl.DeviceIdType.MESH
bf16, f32 = jnp.bfloat16, jnp.float32

LOSS_SCALE = 1024.0
PHYSICS_SHARE = 0.5
RANKS = 8
SIDE = 4
LANES = 128
BLOCK = 256
NT = (((1,), (1,)), ((), ()))
TN = (((0,), (0,)), ((), ()))


def sigmoid(v):
    return 0.5 + 0.5 * jnp.tanh(0.5 * v)


def wide(i, size):
    return pl.ds(pl.multiple_of(i * size, size), size)


def kernel(
    field, wind, w_in, w_mid, w_out, targets, cmap, batch,
    field_out, grad_mid, grad_out,
    ext, gust, mids, win, wint, wout, goal, first, firsts, second, slope, pred, inputs,
    step, outgoing, mine, cnt_out, cnt_in, sum_out, sum_in,
    part, got_x, got_y, half, got_h, final, got_f,
    load_sem, mid_sem, halo_s, halo_r, in_s, in_r, cnt_s, cnt_r, sum_s, sum_r,
    m_s, m_r, one_s, one_r, two_s, two_r, fin_s, fin_r,
):
    grp, lon = lax.axis_index("grp"), lax.axis_index("lon")
    place, zh = lax.div(lon, 2), lax.rem(lon, 2)
    x, y = lax.div(place, SIDE), lax.rem(place, SIDE)
    rank = zh * 4 + grp
    is_trainer = grp == 3

    def rank_at(k):
        return lax.rem(rank + k, RANKS)

    def ring(k):
        other = rank_at(k)
        return (lax.rem(other, 4), place * 2 + lax.div(other, 4))

    def plane(k):
        return (grp, lax.rem(place + k, SIDE * SIDE) * 2 + zh)

    def along_x(k):
        return (grp, lax.rem(x + k, SIDE) * (2 * SIDE) + y * 2 + zh)

    def along_y(k):
        return (grp, x * (2 * SIDE) + lax.rem(y + k, SIDE) * 2 + zh)

    def beside(dg, dl):
        return (lax.rem(grp + dg + 4, 4), lax.rem(lon + dl + 32, 32))

    def remote(src, dst, send, recv, to):
        return pltpu.make_async_remote_copy(
            src_ref=src, dst_ref=dst, send_sem=send, recv_sem=recv,
            device_id=to, device_id_type=MESH,
        )

    loads = [
        pltpu.make_async_copy(field, ext.at[2:6, 8:40], load_sem.at[0]),
        pltpu.make_async_copy(w_in, win, load_sem.at[1]),
        pltpu.make_async_copy(wind, gust.at[1:5, 8:40], load_sem.at[2]),
        pltpu.make_async_copy(w_out, wout, load_sem.at[3]),
        pltpu.make_async_copy(targets, goal, load_sem.at[4]),
    ]

    def mid_load(c):
        return pltpu.make_async_copy(w_mid.at[:, wide(c, BLOCK)], mids.at[c], mid_sem.at[c])

    for load in loads:
        load.start()
    for c in range(RANKS):
        mid_load(c).start()

    barrier = pltpu.get_barrier_semaphore()
    greeted = [ring(k) for k in range(1, RANKS)] + [plane(k) for k in range(1, SIDE * SIDE)]
    far = 2 * zh - 1
    greeted += [beside(dg, far) for dg in (-1, 0, 1)]
    for other in greeted:
        pl.semaphore_signal(barrier, inc=1, device_id=other, device_id_type=MESH)

    names = jnp.broadcast_to(cmap[...].astype(f32), (LANES, LANES)).T
    ids = lax.broadcasted_iota(jnp.int32, (LANES, LANES), 1).astype(f32)
    match = (names == ids).astype(f32)
    own_count = jnp.sum(match, 0, keepdims=True) * jnp.where(is_trainer, 0.0, 1.0)
    cnt_out[...] = jnp.broadcast_to(own_count, (8, LANES))

    loads[0].wait()
    own_in = ext[2:6, 8:40].reshape(LANES, LANES).astype(bf16)
    inputs[wide(rank, LANES), :] = own_in
    loads[2].wait()
    pl.semaphore_wait(barrier, len(greeted))

    in_copies = [
        remote(
            inputs.at[wide(rank, LANES)], inputs.at[wide(rank, LANES)],
            in_s.at[k], in_r.at[k], ring(k),
        ) for k in range(1, RANKS)
    ]
    cnt_copies = [
        remote(cnt_out, cnt_in.at[k], cnt_s.at[k], cnt_r.at[k], ring(k)) for k in range(1, RANKS)
    ]
    halo = [
        (ext.at[2:4, 8:40], ext.at[6:8, 8:40], -1, 0),
        (ext.at[4:6, 8:40], ext.at[0:2, 8:40], 1, 0),
        (ext.at[2:6, 8:16], ext.at[2:6, 40:48], 0, -1),
        (ext.at[2:6, 32:40], ext.at[2:6, 0:8], 0, 1),
        (ext.at[2:3, 8:16], ext.at[6:7, 40:48], -1, -1),
        (ext.at[2:3, 32:40], ext.at[6:7, 0:8], -1, 1),
        (ext.at[5:6, 8:16], ext.at[1:2, 40:48], 1, -1),
        (ext.at[5:6, 32:40], ext.at[1:2, 0:8], 1, 1),
        (gust.at[1:2, 8:40], gust.at[5:6, 8:40], -1, 0),
        (gust.at[4:5, 8:40], gust.at[0:1, 8:40], 1, 0),
        (gust.at[1:5, 8:16], gust.at[1:5, 40:48], 0, -1),
        (gust.at[1:5, 32:40], gust.at[1:5, 0:8], 0, 1),
    ]
    halo_copies = [
        remote(src, dst, halo_s.at[i], halo_r.at[i], beside(dg, dl))
        for i, (src, dst, dg, dl) in enumerate(halo)
    ]
    for copy in cnt_copies + halo_copies + in_copies:
        copy.start()

    loads[1].wait()
    own_in = inputs[wide(rank, LANES), :]

    def first_step(c, carry):
        pre = jnp.dot(own_in, win[:, wide(c, 512)], preferred_element_type=f32)
        first[:, wide(c, 512)] = (pre * sigmoid(pre)).astype(bf16)
        return carry

    lax.fori_loop(0, 4, first_step, 0)
    loads[3].wait()
    pred[...] = jnp.zeros_like(pred)

    def second_step(c, carry):
        mid_load(c).wait()
        pre = jnp.dot(first[...], mids[c], preferred_element_type=f32)
        sig = sigmoid(pre)
        act = (pre * sig).astype(bf16)
        second[:, wide(c, BLOCK)] = act
        slope[:, wide(c, BLOCK)] = sig * (1.0 + pre * (1.0 - sig))
        pred[...] += jnp.dot(act, wout[wide(c, BLOCK), :], preferred_element_type=f32)
        return carry

    lax.fori_loop(0, 4, second_step, 0)

    total = cnt_out[...]
    for k in range(1, RANKS):
        cnt_copies[k - 1].wait_recv()
        total = total + cnt_in[k]
    sum_out[...] = total
    sum_copies = [
        remote(sum_out, sum_in.at[k], sum_s.at[k], sum_r.at[k], plane(k))
        for k in range(1, SIDE * SIDE)
    ]
    for copy in sum_copies:
        copy.start()

    lax.fori_loop(4, RANKS, second_step, 0)

    for copy in halo_copies:
        copy.wait_recv()
    low, high = grp == 0, grp == 2

    def masked(row, values):
        if row < 0:
            return jnp.where(low, 0.0, values)
        if row > 3:
            return jnp.where(high, 0.0, values)
        return values

    def advanced(c, n, s, e, w, u):
        return c - 0.25 * u * (e - w) + 0.15 * (e + w + n + s - 4.0 * c)

    for row in range(-1, 5):
        i = row + 2
        c = masked(row, ext[i, 7:41])
        e, w = masked(row, ext[i, 8:42]), masked(row, ext[i, 6:40])
        n, s = masked(row + 1, ext[i + 1, 7:41]), masked(row - 1, ext[i - 1, 7:41])
        step[row + 1, 7:41] = masked(row, advanced(c, n, s, e, w, gust[row + 1, 7:41]))
    current = []
    for row in range(4):
        c = step[row + 1, 8:40]
        e, w = step[row + 1, 9:41], step[row + 1, 7:39]
        n, s = step[row + 2, 8:40], step[row, 8:40]
        current.append(advanced(c, n, s, e, w, gust[row + 1, 8:40]))
    current = jnp.concatenate(current, 0)
    start = ext[2:6, 8:40].reshape(LANES, LANES)
    increment = (current - start).astype(bf16).astype(f32)
    loads[4].wait()
    wanted = jnp.where(is_trainer, goal[...], increment)

    total = sum_out[...]
    for k in range(1, SIDE * SIDE):
        sum_copies[k - 1].wait_recv()
        total = total + sum_in[k]
    valid = batch[...].astype(f32)
    weight = LOSS_SCALE / (32.0 * (valid + total[0:1, 0:32]))
    column_weight = jnp.sum(match[:, 0:32] * weight, 1, keepdims=True)
    own = lax.broadcasted_iota(jnp.int32, (1, 32), 1) == lon
    own_weight = jnp.sum(jnp.where(own, weight, 0.0), 1, keepdims=True)
    own_valid = jnp.sum(jnp.where(own, valid, 0.0), 1, keepdims=True)
    rows = lax.broadcasted_iota(jnp.int32, (LANES, 1), 0).astype(f32)
    replay_weight = jnp.where(rows < own_valid, own_weight, 0.0)
    row_weight = jnp.where(is_trainer, replay_weight, column_weight)

    predicted = pred[...]
    tendency = predicted.astype(bf16).astype(f32)
    sim = current + PHYSICS_SHARE * tendency
    field_out[...] = jnp.where(is_trainer, predicted, sim).reshape(4, 32, LANES)
    out_slope = ((predicted - wanted) * row_weight).astype(bf16)

    def m_copy(k, h):
        return remote(
            outgoing.at[h, rank_at(k)], mine.at[h, wide(rank, LANES)],
            m_s.at[h, k], m_r.at[h, k], ring(k),
        )

    def mid_step(k, carry):
        t = rank_at(k)
        back = lax.dot_general(out_slope, wout[wide(t, BLOCK), :], NT, preferred_element_type=f32)
        value = (back * slope[:, wide(t, BLOCK)]).astype(bf16)
        outgoing[0, t] = value[:, :LANES]
        outgoing[1, t] = value[:, LANES:]

        @pl.when(k < RANKS)
        def _():
            m_copy(k, 0).start()

        return carry

    lax.fori_loop(1, RANKS + 1, mid_step, 0)
    for k in range(1, RANKS):
        m_copy(k, 1).start()
    for h in range(2):
        mine[h, wide(rank, LANES), :] = outgoing[h, rank]

    def x_copy(q, k):
        return remote(
            part.at[q, 0:2, lax.rem(x + k, SIDE)], got_x.at[q, k],
            one_s.at[q, 0, k], one_r.at[q, 0, k], along_x(k),
        )

    def y_copy(q, k):
        return remote(
            part.at[q, 2:4, :, lax.rem(y + k, SIDE)], got_y.at[q, k],
            one_s.at[q, 1, k], one_r.at[q, 1, k], along_y(k),
        )

    def x2_copy(q, k):
        return remote(
            half.at[q, 0, lax.rem(y + k, SIDE)], got_h.at[q, 0, k],
            two_s.at[q, 0, k], two_r.at[q, 0, k], along_y(k),
        )

    def y2_copy(q, k):
        return remote(
            half.at[q, 1, lax.rem(x + k, SIDE)], got_h.at[q, 1, k],
            two_s.at[q, 1, k], two_r.at[q, 1, k], along_x(k),
        )

    def fin_copy(q, k):
        if q == 0:
            dst = got_f.at[k]
        else:
            dst = grad_mid.at[:, wide(rank * 2 + (q - 1), LANES)]
        return remote(
            final.at[q, rank_at(k)], dst, fin_s.at[q, k], fin_r.at[q, k], ring(k)
        )

    def make_part(q, product):
        def rows_step(c, carry):
            value = product(c).astype(bf16).reshape(2, SIDE, 32, LANES)
            part[q, lax.div(c, 2), pl.ds(lax.rem(c, 2) * 2, 2)] = value
            return carry

        lax.fori_loop(0, 4, rows_step, 0)
        for k in range(1, SIDE):
            x_copy(q, k).start()
        lax.fori_loop(4, 8, rows_step, 0)
        for k in range(1, SIDE):
            y_copy(q, k).start()

    def reduce_one(q):
        total = part[q, 0:2, x].astype(f32)
        for k in range(1, SIDE):
            x_copy(q, k).wait_recv()
            total = total + got_x[q, k].astype(f32)
        total = total.astype(bf16)
        for g in range(2):
            half[q, 0, :, g] = total[g]
        for k in range(1, SIDE):
            x2_copy(q, k).start()
        total = part[q, 2:4, :, y].astype(f32)
        for k in range(1, SIDE):
            y_copy(q, k).wait_recv()
            total = total + got_y[q, k].astype(f32)
        total = total.astype(bf16)
        for g in range(2):
            half[q, 1, :, g] = total[g]
        for k in range(1, SIDE):
            y2_copy(q, k).start()

    def reduce_two(q):
        for axis, own_at, copies in ((0, y, x2_copy), (1, x, y2_copy)):
            total = half[q, axis, own_at].astype(f32)
            for k in range(1, SIDE):
                copies(q, k).wait_recv()
                total = total + got_h[q, axis, k].astype(f32)
            for g in range(2):
                for z in range(2):
                    final[q, z * 4 + axis * 2 + g] = total[g, z * 16 : z * 16 + 16]
        for k in range(1, RANKS):
            fin_copy(q, k).start()

    make_part(
        0,
        lambda c: lax.dot_general(
            second[:, wide(c, BLOCK)], out_slope, TN, preferred_element_type=f32
        ),
    )

    for copy in in_copies:
        copy.wait_recv()

    def turn_step(c, carry):
        wint[wide(c, BLOCK), :] = win[:, wide(c, BLOCK)].T
        return carry

    lax.fori_loop(0, RANKS, turn_step, 0)

    def firsts_step(i, carry):
        c, n = lax.div(i, 2), lax.rem(i, 2)
        pre = lax.dot_general(
            wint[wide(c, BLOCK), :], inputs[wide(n, 512), :], NT, preferred_element_type=f32
        )
        firsts[wide(c, BLOCK), wide(n, 512)] = (pre * sigmoid(pre)).astype(bf16)
        return carry

    lax.fori_loop(0, 2 * RANKS, firsts_step, 0)
    reduce_one(0)

    for h in range(2):
        for k in range(1, RANKS):
            m_copy(k, h).wait_recv()
        make_part(
            1 + h,
            lambda c: jnp.dot(firsts[wide(c, BLOCK), :], mine[h], preferred_element_type=f32),
        )
        if h == 0:
            reduce_two(0)
    reduce_one(1)
    reduce_one(2)
    reduce_two(1)
    reduce_two(2)

    total = final[0, rank]
    for k in range(1, RANKS):
        fin_copy(0, k).wait_recv()
        total = total + got_f[k]
    grad_out[...] = total
    for h in range(2):
        grad_mid[:, wide(rank * 2 + h, LANES)] = final[1 + h, rank]
    for h in range(2):
        for k in range(1, RANKS):
            fin_copy(1 + h, k).wait_recv()

    for copy in in_copies + cnt_copies + halo_copies + sum_copies:
        copy.wait_send()
    for h in range(2):
        for k in range(1, RANKS):
            m_copy(k, h).wait_send()
    for q in range(3):
        for k in range(1, SIDE):
            x_copy(q, k).wait_send()
            y_copy(q, k).wait_send()
            x2_copy(q, k).wait_send()
            y2_copy(q, k).wait_send()
        for k in range(1, RANKS):
            fin_copy(q, k).wait_send()


def body(field, wind, w_in, w_mid, w_out, targets, column_map, batch_count):
    vmem = pl.BlockSpec(memory_space=pltpu.VMEM)
    any_place = pl.BlockSpec(memory_space=pl.ANY)
    hid = w_mid.shape[0]
    dma = pltpu.SemaphoreType.DMA
    V = pltpu.VMEM
    return pl.pallas_call(
        kernel,
        out_shape=(
            jax.ShapeDtypeStruct((4, 32, LANES), f32),
            jax.ShapeDtypeStruct((16, hid), f32),
            jax.ShapeDtypeStruct((16, LANES), f32),
        ),
        in_specs=[any_place] * 6 + [vmem] * 2,
        out_specs=(vmem, vmem, vmem),
        scratch_shapes=[
            V((8, 48, LANES), f32),
            V((6, 48, LANES), f32),
            V((RANKS, hid, BLOCK), bf16),
            V((LANES, hid), bf16),
            V((hid, LANES), bf16),
            V((hid, LANES), bf16),
            V((LANES, LANES), f32),
            V((LANES, hid), bf16),
            V((hid, RANKS * LANES), bf16),
            V((LANES, hid), bf16),
            V((LANES, hid), f32),
            V((LANES, LANES), f32),
            V((RANKS * LANES, LANES), bf16),
            V((6, 48, LANES), f32),
            V((2, RANKS, LANES, LANES), bf16),
            V((2, RANKS * LANES, LANES), bf16),
            V((8, LANES), f32),
            V((RANKS, 8, LANES), f32),
            V((8, LANES), f32),
            V((SIDE * SIDE, 8, LANES), f32),
            V((3, 4, SIDE, SIDE, 32, LANES), bf16),
            V((3, SIDE, 2, SIDE, 32, LANES), bf16),
            V((3, SIDE, 2, SIDE, 32, LANES), bf16),
            V((3, 2, SIDE, 2, 32, LANES), bf16),
            V((3, 2, SIDE, 2, 32, LANES), bf16),
            V((3, RANKS, 16, LANES), f32),
            V((RANKS, 16, LANES), f32),
            dma((5,)),
            dma((RANKS,)),
            dma((12,)),
            dma((12,)),
            dma((RANKS,)),
            dma((RANKS,)),
            dma((RANKS,)),
            dma((RANKS,)),
            dma((SIDE * SIDE,)),
            dma((SIDE * SIDE,)),
            dma((2, RANKS)),
            dma((2, RANKS)),
            dma((3, 2, SIDE)),
            dma((3, 2, SIDE)),
            dma((3, 2, SIDE)),
            dma((3, 2, SIDE)),
            dma((3, RANKS)),
            dma((3, RANKS)),
        ],
        compiler_params=pltpu.CompilerParams(
            collective_id=0, has_side_effects=True, vmem_limit_bytes=48 * 1024 * 1024
        ),
        cost_estimate=pl.CostEstimate(
            flops=3_000_000_000, bytes_accessed=12_000_000, transcendentals=3_000_000
        ),
    )(
        field,
        wind,
        w_in,
        w_mid,
        w_out,
        targets,
        column_map.reshape(1, LANES),
        batch_count.reshape(1, 32),
    )


def solution(mesh):
    placed = (
        P("grp", "lon", None),
        P("grp", "lon", None),
        P(),
        P(),
        P(),
        P("lon", None),
        P("grp", "lon", None, None),
        P(),
    )
    return jax.shard_map(
        body,
        mesh=mesh,
        in_specs=placed,
        out_specs=(P("grp", "lon", None), P(("grp", "lon"), None), P(("grp", "lon"), None)),
        check_vma=False,
    )
```

time: 870 us -> 56 us (0.06)
  waiting for transfers between devices: 708 us -> 0 us
  blocking collectives: 67.4 us -> 0 us
  Pallas kernels: 0 us -> 47.2 us
  starting transfers between devices: 20.7 us -> 0 us
  other arithmetic: 18.1 us -> 0 us
  local copies, waits for them, and re-layouts: 24.4 us -> 7.79 us
  matrix products: 16.4 us -> 0 us
  between operations: 14.1 us -> 0.66 us
    unnamed x2 -> x0, waiting for transfers between devices: 707 us -> none
    psum x1 -> x0, blocking collectives: 67.4 us -> none  [body(): lax.psum(jnp.where(is_trainer, 0.0, jnp.sum(matches, 0)), ('grp', 'lon'))]
    pallas_call x0 -> x1, Pallas kernels: none -> 47.2 us  [body(): pl.pallas_call(kernel, out_shape=(jax.ShapeDtypeStruct((4, 32, LANES), f3...]
    ppermute x8 -> x0, starting transfers between devices: 20.7 us -> none  [the longest x4 15.6 us: padded_2(): lax.ppermute(head, axis, [((i + 1) % count, i) for i in range(count)])]
    dot_general x5 -> x0, matrix products: 16.4 us -> none  [the longest x1 8.69 us: body(): lax.dot_general(first_act, mid_slope, (((0,), (0,)), ((), ())), preferred...]
    concatenate x1 -> x0, other arithmetic: 11.9 us -> none  [body(): jnp.concatenate([part_mid, part_out], 1)]
    unnamed x7 -> x17, local copies, waits for them, and re-layouts: 18.9 us -> 7.79 us
  transfers between devices with their start and end apart: 9 -> 0, of which waited for: 3 -> 0; matrix products, arithmetic and copies ran while one was open for 1% -> 0% of each run, Pallas kernels for 0% -> 0%
where the time goes in v2:
time: 56 us; the launch traced here: 55.6 us
  Pallas kernels  47.2 us (84%)
  local copies, waits for them, and re-layouts  7.79 us (14%)
  between operations  0.66 us (1%)
    pallas_call x1, Pallas kernels, body(): pl.pallas_call(kernel, out_shape=(jax.ShapeDtypeStruct((4, 32, LANES), f3...  47.2 us
    unnamed x17, local copies, waits for them, and re-layouts  7.79 us

profile of v2, /device:TPU:1, one launch (start us, length us, event | category | flops | bytes accessed | tf_op | source)
XLA Modules:
  0.0 55.6 jit_solution(8277916878554754202)
XLA Ops:
  0.6 0.0 copy-start
  0.6 1.0 %copy-done = bf16[128,2048]{1,0:T(8,128)(2,1)S(1)} copy-done((bf16[128,2048]{1,0:T(8,128)(2,1)S(1)}, bf16[128,2048]{1,0:T(8,128)(2,1)}, u32[]{:S(2)}) %copy-start) | copy-done | bytes 524312
  1.7 0.0 copy-start.1
  1.7 1.0 %copy-done.1 = bf16[2048,128]{1,0:T(8,128)(2,1)S(1)} copy-done((bf16[2048,128]{1,0:T(8,128)(2,1)S(1)}, bf16[2048,128]{1,0:T(8,128)(2,1)}, u32[]{:S(2)}) %copy-start.1) | copy-done | bytes 524312
  2.7 0.0 copy-start.2
  2.7 0.8 %copy-done.2 = f32[4,32,128]{2,1,0:T(8,128)S(1)} copy-done((f32[4,32,128]{2,1,0:T(8,128)S(1)}, f32[4,32,128]{2,1,0:T(8,128)}, u32[]{:S(2)}) %copy-start.2) | copy-done | bytes 65560
  3.6 0.0 copy-start.3
  3.6 0.8 %copy-done.3 = f32[4,32,128]{2,1,0:T(8,128)S(1)} copy-done((f32[4,32,128]{2,1,0:T(8,128)S(1)}, f32[4,32,128]{2,1,0:T(8,128)}, u32[]{:S(2)}) %copy-start.3) | copy-done | bytes 65560
  4.4 0.0 copy-start.4
  4.4 0.8 %copy-done.4 = f32[128,128]{1,0:T(8,128)S(1)} copy-done((f32[128,128]{1,0:T(8,128)S(1)}, f32[128,128]{1,0:T(8,128)}, u32[]{:S(2)}) %copy-start.4) | copy-done | bytes 65560
  5.2 0.0 copy-start.5
  5.2 0.7 %copy-done.5 = s32[1,1,128,1]{2,3,1,0:T(1,128)S(1)} copy-done((s32[1,1,128,1]{2,3,1,0:T(1,128)S(1)}, s32[1,1,128,1]{2,3,1,0:T(1,128)}, u32[]{:S(2)}) %copy-start.5) | copy-done | bytes 536
  5.9 0.0 copy-start.6
  5.9 0.7 %copy-done.6 = s32[32]{0:T(128)S(1)} copy-done((s32[32]{0:T(128)S(1)}, s32[32]{0:T(128)}, u32[]{:S(2)}) %copy-start.6) | copy-done | bytes 152
  6.5 47.2 %shard_map.103 = (f32[4,32,128]{2,1,0:T(8,128)S(1)}, f32[16,2048]{1,0:T(8,128)S(1)}, f32[16,128]{1,0:T(8,128)S(1)}) custom-call(f32[4,32,128]{2,1,0:T(8,128)S(1)} %copy-done.2, f32[4,32,128]{2,1,0:T(8,128)S(1)} %copy-done.3, bf16[128,2048]{1,0:T(8,128)(2,1)S(1)} %copy-done, bf16[2048,2048]{1,0:T(8,128)(2,1)} %w_mid.1, bf16[2048,128]{1,0:T(8,128)(2,1)S(1)} %copy-done.1, ...), custom_call_target="tpu_custom_call" | custom-call | flops 3000000000 | bytes 12000000 | tf_op jit(solution)/shard_map/pallas_call | solution.py:400
  53.8 0.6 %copy.14 = f32[4,32,128]{2,1,0:T(8,128)} copy(f32[4,32,128]{2,1,0:T(8,128)S(1)} %get-tuple-element.6) | data formatting | bytes 131072
  54.4 0.7 %copy.15 = f32[16,2048]{1,0:T(8,128)} copy(f32[16,2048]{1,0:T(8,128)S(1)} %get-tuple-element.7) | data formatting | bytes 262144
  55.0 0.6 %copy.16 = f32[16,128]{1,0:T(8,128)} copy(f32[16,128]{1,0:T(8,128)S(1)} %get-tuple-element.8) | data formatting | bytes 16384
Async XLA Ops:
  0.6 1.0 %copy-start = (bf16[128,2048]{1,0:T(8,128)(2,1)S(1)}, bf16[128,2048]{1,0:T(8,128)(2,1)}, u32[]{:S(2)}) copy-start(bf16[128,2048]{1,0:T(8,128)(2,1)} %w_in.1) | copy-start | bytes 1572868
  1.7 1.0 %copy-start.1 = (bf16[2048,128]{1,0:T(8,128)(2,1)S(1)}, bf16[2048,128]{1,0:T(8,128)(2,1)}, u32[]{:S(2)}) copy-start(bf16[2048,128]{1,0:T(8,128)(2,1)} %w_out.1) | copy-start | bytes 1572868
  2.7 0.8 %copy-start.2 = (f32[4,32,128]{2,1,0:T(8,128)S(1)}, f32[4,32,128]{2,1,0:T(8,128)}, u32[]{:S(2)}) copy-start(f32[4,32,128]{2,1,0:T(8,128)} %field.1) | copy-start | bytes 196612
  3.6 0.8 %copy-start.3 = (f32[4,32,128]{2,1,0:T(8,128)S(1)}, f32[4,32,128]{2,1,0:T(8,128)}, u32[]{:S(2)}) copy-start(f32[4,32,128]{2,1,0:T(8,128)} %wind.1) | copy-start | bytes 196612
  4.4 0.8 %copy-start.4 = (f32[128,128]{1,0:T(8,128)S(1)}, f32[128,128]{1,0:T(8,128)}, u32[]{:S(2)}) copy-start(f32[128,128]{1,0:T(8,128)} %targets.1) | copy-start | bytes 196612
  5.2 0.7 %copy-start.5 = (s32[1,1,128,1]{2,3,1,0:T(1,128)S(1)}, s32[1,1,128,1]{2,3,1,0:T(1,128)}, u32[]{:S(2)}) copy-start(s32[1,1,128,1]{2,3,1,0:T(1,128)} %param.14) | copy-start | bytes 1540
  5.9 0.7 %copy-start.6 = (s32[32]{0:T(128)S(1)}, s32[32]{0:T(128)}, u32[]{:S(2)}) copy-start(s32[32]{0:T(128)} %param.15) | copy-start | bytes 388

commit v3 on v2

--- a/solution.py
+++ b/solution.py
@@ -14,6 +14,7 @@
 SIDE = 4
 LANES = 128
 BLOCK = 256
+WIDE = 512
 NT = (((1,), (1,)), ((), ()))
 TN = (((0,), (0,)), ((), ()))
 
@@ -29,11 +30,11 @@
 def kernel(
     field, wind, w_in, w_mid, w_out, targets, cmap, batch,
     field_out, grad_mid, grad_out,
-    ext, gust, mids, win, wint, wout, goal, first, firsts, second, slope, pred, inputs,
+    ext, gust, mids, win, wint, wout, goal, first, firsts, second, slope, inputs,
     step, outgoing, mine, cnt_out, cnt_in, sum_out, sum_in,
-    part, got_x, got_y, half, got_h, final, got_f,
+    part, got_x, got_y, half, got_h,
     load_sem, mid_sem, halo_s, halo_r, in_s, in_r, cnt_s, cnt_r, sum_s, sum_r,
-    m_s, m_r, one_s, one_r, two_s, two_r, fin_s, fin_r,
+    m_s, m_r, one_s, one_r, two_s, two_r,
 ):
     grp, lon = lax.axis_index("grp"), lax.axis_index("lon")
     place, zh = lax.div(lon, 2), lax.rem(lon, 2)
@@ -75,11 +76,11 @@
     ]
 
     def mid_load(c):
-        return pltpu.make_async_copy(w_mid.at[:, wide(c, BLOCK)], mids.at[c], mid_sem.at[c])
+        return pltpu.make_async_copy(w_mid.at[:, c * WIDE : c * WIDE + WIDE], mids.at[c], mid_sem.at[c])
 
     for load in loads:
         load.start()
-    for c in range(RANKS):
+    for c in range(4):
         mid_load(c).start()
 
     barrier = pltpu.get_barrier_semaphore()
@@ -134,26 +135,22 @@
     loads[1].wait()
     own_in = inputs[wide(rank, LANES), :]
 
-    def first_step(c, carry):
-        pre = jnp.dot(own_in, win[:, wide(c, 512)], preferred_element_type=f32)
-        first[:, wide(c, 512)] = (pre * sigmoid(pre)).astype(bf16)
-        return carry
-
-    lax.fori_loop(0, 4, first_step, 0)
+    for c in range(4):
+        pre = jnp.dot(own_in, win[:, c * 512 : c * 512 + 512], preferred_element_type=f32)
+        first[:, c * 512 : c * 512 + 512] = (pre * sigmoid(pre)).astype(bf16)
     loads[3].wait()
-    pred[...] = jnp.zeros_like(pred)
-
-    def second_step(c, carry):
+
+    def second_step(c):
         mid_load(c).wait()
+        at = slice(c * WIDE, c * WIDE + WIDE)
         pre = jnp.dot(first[...], mids[c], preferred_element_type=f32)
         sig = sigmoid(pre)
         act = (pre * sig).astype(bf16)
-        second[:, wide(c, BLOCK)] = act
-        slope[:, wide(c, BLOCK)] = sig * (1.0 + pre * (1.0 - sig))
-        pred[...] += jnp.dot(act, wout[wide(c, BLOCK), :], preferred_element_type=f32)
-        return carry
-
-    lax.fori_loop(0, 4, second_step, 0)
+        second[:, at] = act
+        slope[:, at] = sig * (1.0 + pre * (1.0 - sig))
+        return jnp.dot(act, wout[at, :], preferred_element_type=f32)
+
+    predicted = second_step(0) + second_step(1)
 
     total = cnt_out[...]
     for k in range(1, RANKS):
@@ -167,7 +164,7 @@
     for copy in sum_copies:
         copy.start()
 
-    lax.fori_loop(4, RANKS, second_step, 0)
+    predicted = predicted + second_step(2) + second_step(3)
 
     for copy in halo_copies:
         copy.wait_recv()
@@ -201,6 +198,25 @@
     loads[4].wait()
     wanted = jnp.where(is_trainer, goal[...], increment)
 
+    for copy in in_copies:
+        copy.wait_recv()
+
+    def turn_step(c, carry):
+        wint[wide(c, BLOCK), :] = win[:, wide(c, BLOCK)].T
+        return carry
+
+    lax.fori_loop(0, RANKS, turn_step, 0)
+
+    def firsts_step(i, carry):
+        c, n = lax.div(i, 2), lax.rem(i, 2)
+        pre = lax.dot_general(
+            wint[wide(c, BLOCK), :], inputs[wide(n, 512), :], NT, preferred_element_type=f32
+        )
+        firsts[wide(c, BLOCK), wide(n, 512)] = (pre * sigmoid(pre)).astype(bf16)
+        return carry
+
+    lax.fori_loop(0, RANKS, firsts_step, 0)
+
     total = sum_out[...]
     for k in range(1, SIDE * SIDE):
         sum_copies[k - 1].wait_recv()
@@ -215,7 +231,6 @@
     replay_weight = jnp.where(rows < own_valid, own_weight, 0.0)
     row_weight = jnp.where(is_trainer, replay_weight, column_weight)
 
-    predicted = pred[...]
     tendency = predicted.astype(bf16).astype(f32)
     sim = current + PHYSICS_SHARE * tendency
     field_out[...] = jnp.where(is_trainer, predicted, sim).reshape(4, 32, LANES)
@@ -227,20 +242,14 @@
             m_s.at[h, k], m_r.at[h, k], ring(k),
         )
 
-    def mid_step(k, carry):
+    for k in range(1, RANKS + 1):
         t = rank_at(k)
         back = lax.dot_general(out_slope, wout[wide(t, BLOCK), :], NT, preferred_element_type=f32)
         value = (back * slope[:, wide(t, BLOCK)]).astype(bf16)
         outgoing[0, t] = value[:, :LANES]
         outgoing[1, t] = value[:, LANES:]
-
-        @pl.when(k < RANKS)
-        def _():
+        if k < RANKS:
             m_copy(k, 0).start()
-
-        return carry
-
-    lax.fori_loop(1, RANKS + 1, mid_step, 0)
     for k in range(1, RANKS):
         m_copy(k, 1).start()
     for h in range(2):
@@ -258,123 +267,103 @@
             one_s.at[q, 1, k], one_r.at[q, 1, k], along_y(k),
         )
 
-    def x2_copy(q, k):
-        return remote(
-            half.at[q, 0, lax.rem(y + k, SIDE)], got_h.at[q, 0, k],
-            two_s.at[q, 0, k], two_r.at[q, 0, k], along_y(k),
-        )
-
-    def y2_copy(q, k):
-        return remote(
-            half.at[q, 1, lax.rem(x + k, SIDE)], got_h.at[q, 1, k],
-            two_s.at[q, 1, k], two_r.at[q, 1, k], along_x(k),
-        )
-
-    def fin_copy(q, k):
-        if q == 0:
-            dst = got_f.at[k]
+    def out_copy(q, axis, k, g, z):
+        if axis == 0:
+            at = lax.rem(y + k, SIDE)
+            lon_at = x * (2 * SIDE) + at * 2 + z
         else:
-            dst = grad_mid.at[:, wide(rank * 2 + (q - 1), LANES)]
-        return remote(
-            final.at[q, rank_at(k)], dst, fin_s.at[q, k], fin_r.at[q, k], ring(k)
-        )
-
-    def make_part(q, product):
+            at = lax.rem(x + k, SIDE)
+            lon_at = at * (2 * SIDE) + y * 2 + z
+        src, dst = half.at[q, axis, at, g, z], got_h.at[q, k * RANKS + rank]
+        return remote(src, dst, two_s.at[q], two_r.at[q], (2 * axis + g, lon_at))
+
+    def own_copy(q, axis, g, z):
+        src = half.at[q, axis, y if axis == 0 else x, g, z]
+        return pltpu.make_async_copy(src, got_h.at[q, rank], two_r.at[q])
+
+    def send_out(q, axis):
+        for g in range(2):
+            for z in range(2):
+                here = (grp == 2 * axis + g) & (zh == z)
+                for k in range(1, SIDE):
+                    out_copy(q, axis, k, g, z).start()
+
+                @pl.when(here)
+                def _():
+                    own_copy(q, axis, g, z).start()
+
+                @pl.when(jnp.logical_not(here))
+                def _():
+                    out_copy(q, axis, 0, g, z).start()
+
+    def out_all(q):
+        return remote(got_h.at[q], got_h.at[q], two_s.at[q], two_r.at[q], ring(1))
+
+    def make_part(q, size, product):
+        steps = 1024 // size
+
         def rows_step(c, carry):
-            value = product(c).astype(bf16).reshape(2, SIDE, 32, LANES)
-            part[q, lax.div(c, 2), pl.ds(lax.rem(c, 2) * 2, 2)] = value
+            value = product(c).astype(bf16)
+            if size == 1024:
+                part[q, pl.ds(c * 2, 2)] = value.reshape(2, SIDE, SIDE, 32, LANES)
+            else:
+                at = pl.ds(lax.rem(c, 2) * 2, 2)
+                part[q, lax.div(c, 2), at] = value.reshape(2, SIDE, 32, LANES)
             return carry
 
-        lax.fori_loop(0, 4, rows_step, 0)
+        lax.fori_loop(0, steps, rows_step, 0)
         for k in range(1, SIDE):
             x_copy(q, k).start()
-        lax.fori_loop(4, 8, rows_step, 0)
+        lax.fori_loop(steps, 2 * steps, rows_step, 0)
         for k in range(1, SIDE):
             y_copy(q, k).start()
 
     def reduce_one(q):
-        total = part[q, 0:2, x].astype(f32)
-        for k in range(1, SIDE):
-            x_copy(q, k).wait_recv()
-            total = total + got_x[q, k].astype(f32)
-        total = total.astype(bf16)
-        for g in range(2):
-            half[q, 0, :, g] = total[g]
-        for k in range(1, SIDE):
-            x2_copy(q, k).start()
-        total = part[q, 2:4, :, y].astype(f32)
-        for k in range(1, SIDE):
-            y_copy(q, k).wait_recv()
-            total = total + got_y[q, k].astype(f32)
-        total = total.astype(bf16)
-        for g in range(2):
-            half[q, 1, :, g] = total[g]
-        for k in range(1, SIDE):
-            y2_copy(q, k).start()
-
-    def reduce_two(q):
-        for axis, own_at, copies in ((0, y, x2_copy), (1, x, y2_copy)):
-            total = half[q, axis, own_at].astype(f32)
+        for axis in range(2):
+            if axis == 0:
+                total, copies, got = part[q, 0:2, x], x_copy, got_x
+            else:
+                total, copies, got = part[q, 2:4, :, y], y_copy, got_y
+            total = total.astype(f32)
             for k in range(1, SIDE):
                 copies(q, k).wait_recv()
-                total = total + got_h[q, axis, k].astype(f32)
+                total = total + got[q, k].astype(f32)
+            total = total.astype(bf16).reshape(2, SIDE, 2, 16, LANES)
             for g in range(2):
-                for z in range(2):
-                    final[q, z * 4 + axis * 2 + g] = total[g, z * 16 : z * 16 + 16]
-        for k in range(1, RANKS):
-            fin_copy(q, k).start()
+                half[q, axis, :, g] = total[g]
+            send_out(q, axis)
 
     make_part(
         0,
+        BLOCK,
         lambda c: lax.dot_general(
             second[:, wide(c, BLOCK)], out_slope, TN, preferred_element_type=f32
         ),
     )
 
-    for copy in in_copies:
-        copy.wait_recv()
-
-    def turn_step(c, carry):
-        wint[wide(c, BLOCK), :] = win[:, wide(c, BLOCK)].T
-        return carry
-
-    lax.fori_loop(0, RANKS, turn_step, 0)
-
-    def firsts_step(i, carry):
-        c, n = lax.div(i, 2), lax.rem(i, 2)
-        pre = lax.dot_general(
-            wint[wide(c, BLOCK), :], inputs[wide(n, 512), :], NT, preferred_element_type=f32
-        )
-        firsts[wide(c, BLOCK), wide(n, 512)] = (pre * sigmoid(pre)).astype(bf16)
-        return carry
-
-    lax.fori_loop(0, 2 * RANKS, firsts_step, 0)
-    reduce_one(0)
-
+    lax.fori_loop(RANKS, 2 * RANKS, firsts_step, 0)
     for h in range(2):
         for k in range(1, RANKS):
             m_copy(k, h).wait_recv()
         make_part(
             1 + h,
-            lambda c: jnp.dot(firsts[wide(c, BLOCK), :], mine[h], preferred_element_type=f32),
+            1024,
+            lambda c: jnp.dot(firsts[wide(c, 1024), :], mine[h], preferred_element_type=f32),
         )
         if h == 0:
-            reduce_two(0)
+            reduce_one(0)
     reduce_one(1)
     reduce_one(2)
-    reduce_two(1)
-    reduce_two(2)
-
-    total = final[0, rank]
-    for k in range(1, RANKS):
-        fin_copy(0, k).wait_recv()
-        total = total + got_f[k]
-    grad_out[...] = total
+
+    out_all(0).wait_recv()
+    grad_out[...] = jnp.sum(got_h[0].astype(f32), 0)
     for h in range(2):
-        grad_mid[:, wide(rank * 2 + h, LANES)] = final[1 + h, rank]
-    for h in range(2):
-        for k in range(1, RANKS):
-            fin_copy(1 + h, k).wait_recv()
+        out_all(1 + h).wait_recv()
+        got = got_h[1 + h].astype(f32).reshape(SIDE, RANKS, 16, LANES)
+        total = jnp.sum(got, 0)
+        for t in range(RANKS):
+            at = t * BLOCK + h * LANES
+            grad_mid[:, at : at + LANES] = total[t]
 
     for copy in in_copies + cnt_copies + halo_copies + sum_copies:
         copy.wait_send()
@@ -385,10 +374,8 @@
         for k in range(1, SIDE):
             x_copy(q, k).wait_send()
             y_copy(q, k).wait_send()
-            x2_copy(q, k).wait_send()
-            y2_copy(q, k).wait_send()
-        for k in range(1, RANKS):
-            fin_copy(q, k).wait_send()
+        sent = got_h.at[q, 1:]
+        remote(sent, sent, two_s.at[q], two_r.at[q], ring(1)).wait_send()
 
 
 def body(field, wind, w_in, w_mid, w_out, targets, column_map, batch_count):
@@ -409,7 +396,7 @@
         scratch_shapes=[
             V((8, 48, LANES), f32),
             V((6, 48, LANES), f32),
-            V((RANKS, hid, BLOCK), bf16),
+            V((4, hid, WIDE), bf16),
             V((LANES, hid), bf16),
             V((hid, LANES), bf16),
             V((hid, LANES), bf16),
@@ -418,7 +405,6 @@
             V((hid, RANKS * LANES), bf16),
             V((LANES, hid), bf16),
             V((LANES, hid), f32),
-            V((LANES, LANES), f32),
             V((RANKS * LANES, LANES), bf16),
             V((6, 48, LANES), f32),
             V((2, RANKS, LANES, LANES), bf16),
@@ -430,12 +416,10 @@
             V((3, 4, SIDE, SIDE, 32, LANES), bf16),
             V((3, SIDE, 2, SIDE, 32, LANES), bf16),
             V((3, SIDE, 2, SIDE, 32, LANES), bf16),
-            V((3, 2, SIDE, 2, 32, LANES), bf16),
-            V((3, 2, SIDE, 2, 32, LANES), bf16),
-            V((3, RANKS, 16, LANES), f32),
-            V((RANKS, 16, LANES), f32),
+            V((3, 2, SIDE, 2, 2, 16, LANES), bf16),
+            V((3, SIDE * RANKS, 16, LANES), bf16),
             dma((5,)),
-            dma((RANKS,)),
+            dma((4,)),
             dma((12,)),
             dma((12,)),
             dma((RANKS,)),
@@ -448,13 +432,11 @@
             dma((2, RANKS)),
             dma((3, 2, SIDE)),
             dma((3, 2, SIDE)),
-            dma((3, 2, SIDE)),
-            dma((3, 2, SIDE)),
-            dma((3, RANKS)),
-            dma((3, RANKS)),
+            dma((3,)),
+            dma((3,)),
         ],
         compiler_params=pltpu.CompilerParams(
-            collective_id=0, has_side_effects=True, vmem_limit_bytes=48 * 1024 * 1024
+            collective_id=0, has_side_effects=True, vmem_limit_bytes=64 * 1024 * 1024
         ),
         cost_estimate=pl.CostEstimate(
             flops=3_000_000_000, bytes_accessed=12_000_000, transcendentals=3_000_000

time: 56 us -> 48.1 us (0.86)
  Pallas kernels: 47.2 us -> 42.9 us
  local copies, waits for them, and re-layouts: 7.79 us -> 4.34 us
    pallas_call x1, Pallas kernels: 47.2 us -> 42.9 us  [body(): pl.pallas_call(kernel, out_shape=(jax.ShapeDtypeStruct((4, 32, LANES), f3...]
    unnamed x17 -> x3, local copies, waits for them, and re-layouts: 7.79 us -> 4.34 us
where the time goes in v3:
time: 48.1 us; the launch traced here: 47.9 us
  Pallas kernels  42.9 us (89%)
  local copies, waits for them, and re-layouts  4.34 us (9%)
  between operations  0.64 us (1%)
    pallas_call x1, Pallas kernels, body(): pl.pallas_call(kernel, out_shape=(jax.ShapeDtypeStruct((4, 32, LANES), f3...  42.9 us
    unnamed x3, local copies, waits for them, and re-layouts  4.34 us

profile of v3, /device:TPU:1, one launch (start us, length us, event | category | flops | bytes accessed | tf_op | source)
XLA Modules:
  0.0 47.9 jit_solution(5396969630867577256)
XLA Ops:
  0.6 42.9 %shard_map.103 = (f32[4,32,128]{2,1,0:T(8,128)}, f32[16,2048]{1,0:T(8,128)}, f32[16,128]{1,0:T(8,128)}) custom-call(f32[4,32,128]{2,1,0:T(8,128)} %field.1, f32[4,32,128]{2,1,0:T(8,128)} %wind.1, bf16[128,2048]{1,0:T(8,128)(2,1)} %w_in.1, bf16[2048,2048]{1,0:T(8,128)(2,1)} %w_mid.1, bf16[2048,128]{1,0:T(8,128)(2,1)} %w_out.1, f32[128,128]{1,0:T(8,128)} %targets.1, ...), custom_call_target="tpu_custom_call" | custom-call | flops 3000000000 | bytes 12000000 | tf_op jit(solution)/shard_map/pallas_call | solution.py:387
  43.5 1.5 %copy.14 = f32[4,32,128]{2,1,0:T(8,128)} copy(f32[4,32,128]{2,1,0:T(8,128)} %get-tuple-element.6) | data formatting | bytes 131072
  45.0 1.6 %copy.15 = f32[16,2048]{1,0:T(8,128)} copy(f32[16,2048]{1,0:T(8,128)} %get-tuple-element.7) | data formatting | bytes 262144
  46.6 1.3 %copy.16 = f32[16,128]{1,0:T(8,128)} copy(f32[16,128]{1,0:T(8,128)} %get-tuple-element.8) | data formatting | bytes 16384

commit v4 on v3

--- a/solution.py
+++ b/solution.py
@@ -13,6 +13,7 @@
 RANKS = 8
 SIDE = 4
 LANES = 128
+VMEM_BYTES = 62 * 1024 * 1024
 BLOCK = 256
 WIDE = 512
 NT = (((1,), (1,)), ((), ()))
@@ -28,11 +29,11 @@
 
 
 def kernel(
-    field, wind, w_in, w_mid, w_out, targets, cmap, batch,
+    field, wind, w_in, w_mid, w_out, targets, cmap_in, batch_in,
     field_out, grad_mid, grad_out,
-    ext, gust, mids, win, wint, wout, goal, first, firsts, second, slope, inputs,
+    cmap, batch, ext, gust, mids, win, wint, wout, goal, first, firsts, second, slope, inputs,
     step, outgoing, mine, cnt_out, cnt_in, sum_out, sum_in,
-    part, got_x, got_y, half, got_h,
+    part, got_one, half, got_h,
     load_sem, mid_sem, halo_s, halo_r, in_s, in_r, cnt_s, cnt_r, sum_s, sum_r,
     m_s, m_r, one_s, one_r, two_s, two_r,
 ):
@@ -73,23 +74,28 @@
         pltpu.make_async_copy(wind, gust.at[1:5, 8:40], load_sem.at[2]),
         pltpu.make_async_copy(w_out, wout, load_sem.at[3]),
         pltpu.make_async_copy(targets, goal, load_sem.at[4]),
+        pltpu.make_async_copy(cmap_in, cmap, load_sem.at[5]),
+        pltpu.make_async_copy(batch_in, batch, load_sem.at[6]),
     ]
 
     def mid_load(c):
         return pltpu.make_async_copy(w_mid.at[:, c * WIDE : c * WIDE + WIDE], mids.at[c], mid_sem.at[c])
 
-    for load in loads:
-        load.start()
+    barrier = pltpu.get_barrier_semaphore()
+    far = 2 * zh - 1
+    greeted = [beside(dg, far) for dg in (-1, 0, 1)]
+    greeted += [plane(k) for k in range(1, SIDE * SIDE)] + [ring(k) for k in range(1, RANKS)]
+    for other in greeted:
+        pl.semaphore_signal(barrier, inc=1, device_id=other, device_id_type=MESH)
+
+    for i in (0, 2, 5, 1):
+        loads[i].start()
     for c in range(4):
         mid_load(c).start()
-
-    barrier = pltpu.get_barrier_semaphore()
-    greeted = [ring(k) for k in range(1, RANKS)] + [plane(k) for k in range(1, SIDE * SIDE)]
-    far = 2 * zh - 1
-    greeted += [beside(dg, far) for dg in (-1, 0, 1)]
-    for other in greeted:
-        pl.semaphore_signal(barrier, inc=1, device_id=other, device_id_type=MESH)
-
+    for i in (3, 4, 6):
+        loads[i].start()
+
+    loads[5].wait()
     names = jnp.broadcast_to(cmap[...].astype(f32), (LANES, LANES)).T
     ids = lax.broadcasted_iota(jnp.int32, (LANES, LANES), 1).astype(f32)
     match = (names == ids).astype(f32)
@@ -129,7 +135,7 @@
         remote(src, dst, halo_s.at[i], halo_r.at[i], beside(dg, dl))
         for i, (src, dst, dg, dl) in enumerate(halo)
     ]
-    for copy in cnt_copies + halo_copies + in_copies:
+    for copy in halo_copies + cnt_copies + in_copies:
         copy.start()
 
     loads[1].wait()
@@ -165,6 +171,12 @@
         copy.start()
 
     predicted = predicted + second_step(2) + second_step(3)
+
+    def turn_step(c, carry):
+        wint[wide(c, BLOCK), :] = win[:, wide(c, BLOCK)].T
+        return carry
+
+    lax.fori_loop(0, RANKS, turn_step, 0)
 
     for copy in halo_copies:
         copy.wait_recv()
@@ -198,29 +210,11 @@
     loads[4].wait()
     wanted = jnp.where(is_trainer, goal[...], increment)
 
-    for copy in in_copies:
-        copy.wait_recv()
-
-    def turn_step(c, carry):
-        wint[wide(c, BLOCK), :] = win[:, wide(c, BLOCK)].T
-        return carry
-
-    lax.fori_loop(0, RANKS, turn_step, 0)
-
-    def firsts_step(i, carry):
-        c, n = lax.div(i, 2), lax.rem(i, 2)
-        pre = lax.dot_general(
-            wint[wide(c, BLOCK), :], inputs[wide(n, 512), :], NT, preferred_element_type=f32
-        )
-        firsts[wide(c, BLOCK), wide(n, 512)] = (pre * sigmoid(pre)).astype(bf16)
-        return carry
-
-    lax.fori_loop(0, RANKS, firsts_step, 0)
-
     total = sum_out[...]
     for k in range(1, SIDE * SIDE):
         sum_copies[k - 1].wait_recv()
         total = total + sum_in[k]
+    loads[6].wait()
     valid = batch[...].astype(f32)
     weight = LOSS_SCALE / (32.0 * (valid + total[0:1, 0:32]))
     column_weight = jnp.sum(match[:, 0:32] * weight, 1, keepdims=True)
@@ -242,30 +236,36 @@
             m_s.at[h, k], m_r.at[h, k], ring(k),
         )
 
-    for k in range(1, RANKS + 1):
-        t = rank_at(k)
-        back = lax.dot_general(out_slope, wout[wide(t, BLOCK), :], NT, preferred_element_type=f32)
-        value = (back * slope[:, wide(t, BLOCK)]).astype(bf16)
-        outgoing[0, t] = value[:, :LANES]
-        outgoing[1, t] = value[:, LANES:]
-        if k < RANKS:
-            m_copy(k, 0).start()
-    for k in range(1, RANKS):
+    for group in ((4, 3, 5, 2), (6, 1, 7, 0)):
+        for k in group:
+            t = rank_at(k)
+            back = lax.dot_general(
+                out_slope, wout[wide(t, BLOCK), :], NT, preferred_element_type=f32
+            )
+            value = (back * slope[:, wide(t, BLOCK)]).astype(bf16)
+            outgoing[0, t] = value[:, :LANES]
+            outgoing[1, t] = value[:, LANES:]
+        for k in group:
+            if k:
+                m_copy(k, 0).start()
+    for k in (4, 3, 5, 2, 6, 1, 7):
         m_copy(k, 1).start()
     for h in range(2):
         mine[h, wide(rank, LANES), :] = outgoing[h, rank]
 
-    def x_copy(q, k):
+    def one_copy(q, k, g):
+        if g < 2:
+            src, to = part.at[q, g, lax.rem(x + k, SIDE)], along_x(k)
+        else:
+            src, to = part.at[q, g, :, lax.rem(y + k, SIDE)], along_y(k)
+        axis = g // 2
         return remote(
-            part.at[q, 0:2, lax.rem(x + k, SIDE)], got_x.at[q, k],
-            one_s.at[q, 0, k], one_r.at[q, 0, k], along_x(k),
+            src, got_one.at[q, axis, k, g % 2], one_s.at[q, axis, k], one_r.at[q, axis, k], to
         )
 
-    def y_copy(q, k):
-        return remote(
-            part.at[q, 2:4, :, lax.rem(y + k, SIDE)], got_y.at[q, k],
-            one_s.at[q, 1, k], one_r.at[q, 1, k], along_y(k),
-        )
+    def one_pair(q, axis, k):
+        both = got_one.at[q, axis, k]
+        return remote(both, both, one_s.at[q, axis, k], one_r.at[q, axis, k], along_x(k))
 
     def out_copy(q, axis, k, g, z):
         if axis == 0:
@@ -282,52 +282,37 @@
         return pltpu.make_async_copy(src, got_h.at[q, rank], two_r.at[q])
 
     def send_out(q, axis):
-        for g in range(2):
-            for z in range(2):
-                here = (grp == 2 * axis + g) & (zh == z)
-                for k in range(1, SIDE):
-                    out_copy(q, axis, k, g, z).start()
-
-                @pl.when(here)
-                def _():
-                    own_copy(q, axis, g, z).start()
-
-                @pl.when(jnp.logical_not(here))
-                def _():
-                    out_copy(q, axis, 0, g, z).start()
+        rows = [(g, z) for g in range(2) for z in range(2)]
+        for k in (2, 1, 3):
+            for g, z in rows:
+                out_copy(q, axis, k, g, z).start()
+        for g, z in rows:
+            here = (grp == 2 * axis + g) & (zh == z)
+
+            @pl.when(here)
+            def _():
+                own_copy(q, axis, g, z).start()
+
+            @pl.when(jnp.logical_not(here))
+            def _():
+                out_copy(q, axis, 0, g, z).start()
 
     def out_all(q):
         return remote(got_h.at[q], got_h.at[q], two_s.at[q], two_r.at[q], ring(1))
 
-    def make_part(q, size, product):
-        steps = 1024 // size
-
-        def rows_step(c, carry):
-            value = product(c).astype(bf16)
-            if size == 1024:
-                part[q, pl.ds(c * 2, 2)] = value.reshape(2, SIDE, SIDE, 32, LANES)
-            else:
-                at = pl.ds(lax.rem(c, 2) * 2, 2)
-                part[q, lax.div(c, 2), at] = value.reshape(2, SIDE, 32, LANES)
-            return carry
-
-        lax.fori_loop(0, steps, rows_step, 0)
-        for k in range(1, SIDE):
-            x_copy(q, k).start()
-        lax.fori_loop(steps, 2 * steps, rows_step, 0)
-        for k in range(1, SIDE):
-            y_copy(q, k).start()
+    def make_part(q, product):
+        for g in (0, 2, 1, 3):
+            part[q, g] = product(g).astype(bf16).reshape(SIDE, SIDE, 32, LANES)
+            for k in (2, 1, 3):
+                one_copy(q, k, g).start()
 
     def reduce_one(q):
         for axis in range(2):
-            if axis == 0:
-                total, copies, got = part[q, 0:2, x], x_copy, got_x
-            else:
-                total, copies, got = part[q, 2:4, :, y], y_copy, got_y
+            total = part[q, 0:2, x] if axis == 0 else part[q, 2:4, :, y]
             total = total.astype(f32)
             for k in range(1, SIDE):
-                copies(q, k).wait_recv()
-                total = total + got[q, k].astype(f32)
+                one_pair(q, axis, k).wait_recv()
+                total = total + got_one[q, axis, k].astype(f32)
             total = total.astype(bf16).reshape(2, SIDE, 2, 16, LANES)
             for g in range(2):
                 half[q, axis, :, g] = total[g]
@@ -335,25 +320,35 @@
 
     make_part(
         0,
-        BLOCK,
-        lambda c: lax.dot_general(
-            second[:, wide(c, BLOCK)], out_slope, TN, preferred_element_type=f32
+        lambda g: lax.dot_general(
+            second[:, g * 512 : g * 512 + 512], out_slope, TN, preferred_element_type=f32
         ),
     )
 
-    lax.fori_loop(RANKS, 2 * RANKS, firsts_step, 0)
+    for copy in in_copies:
+        copy.wait_recv()
+
+    def firsts_step(i, carry):
+        c, n = lax.div(i, 2), lax.rem(i, 2)
+        pre = lax.dot_general(
+            wint[wide(c, BLOCK), :], inputs[wide(n, 512), :], NT, preferred_element_type=f32
+        )
+        firsts[wide(c, BLOCK), wide(n, 512)] = (pre * sigmoid(pre)).astype(bf16)
+        return carry
+
+    lax.fori_loop(0, 2 * RANKS, firsts_step, 0)
+
     for h in range(2):
         for k in range(1, RANKS):
             m_copy(k, h).wait_recv()
         make_part(
             1 + h,
-            1024,
-            lambda c: jnp.dot(firsts[wide(c, 1024), :], mine[h], preferred_element_type=f32),
+            lambda g: jnp.dot(
+                firsts[g * 512 : g * 512 + 512, :], mine[h], preferred_element_type=f32
+            ),
         )
-        if h == 0:
-            reduce_one(0)
-    reduce_one(1)
-    reduce_one(2)
+    for q in range(3):
+        reduce_one(q)
 
     out_all(0).wait_recv()
     grad_out[...] = jnp.sum(got_h[0].astype(f32), 0)
@@ -372,28 +367,34 @@
             m_copy(k, h).wait_send()
     for q in range(3):
         for k in range(1, SIDE):
-            x_copy(q, k).wait_send()
-            y_copy(q, k).wait_send()
+            for axis in range(2):
+                one_pair(q, axis, k).wait_send()
         sent = got_h.at[q, 1:]
         remote(sent, sent, two_s.at[q], two_r.at[q], ring(1)).wait_send()
 
 
+def hand_on(a, b, c, a_out, b_out, c_out):
+    a_out[...], b_out[...], c_out[...] = a[...], b[...], c[...]
+
+
 def body(field, wind, w_in, w_mid, w_out, targets, column_map, batch_count):
     vmem = pl.BlockSpec(memory_space=pltpu.VMEM)
-    any_place = pl.BlockSpec(memory_space=pl.ANY)
+    hbm = pl.BlockSpec(memory_space=pltpu.HBM)
     hid = w_mid.shape[0]
     dma = pltpu.SemaphoreType.DMA
     V = pltpu.VMEM
-    return pl.pallas_call(
+    results = pl.pallas_call(
         kernel,
         out_shape=(
             jax.ShapeDtypeStruct((4, 32, LANES), f32),
             jax.ShapeDtypeStruct((16, hid), f32),
             jax.ShapeDtypeStruct((16, LANES), f32),
         ),
-        in_specs=[any_place] * 6 + [vmem] * 2,
+        in_specs=[hbm] * 8,
         out_specs=(vmem, vmem, vmem),
         scratch_shapes=[
+            V((1, LANES), jnp.int32),
+            V((1, 32), jnp.int32),
             V((8, 48, LANES), f32),
             V((6, 48, LANES), f32),
             V((4, hid, WIDE), bf16),
@@ -414,11 +415,10 @@
             V((8, LANES), f32),
             V((SIDE * SIDE, 8, LANES), f32),
             V((3, 4, SIDE, SIDE, 32, LANES), bf16),
-            V((3, SIDE, 2, SIDE, 32, LANES), bf16),
-            V((3, SIDE, 2, SIDE, 32, LANES), bf16),
+            V((3, 2, SIDE, 2, SIDE, 32, LANES), bf16),
             V((3, 2, SIDE, 2, 2, 16, LANES), bf16),
             V((3, SIDE * RANKS, 16, LANES), bf16),
-            dma((5,)),
+            dma((7,)),
             dma((4,)),
             dma((12,)),
             dma((12,)),
@@ -436,7 +436,7 @@
             dma((3,)),
         ],
         compiler_params=pltpu.CompilerParams(
-            collective_id=0, has_side_effects=True, vmem_limit_bytes=64 * 1024 * 1024
+            collective_id=0, has_side_effects=True, vmem_limit_bytes=VMEM_BYTES
         ),
         cost_estimate=pl.CostEstimate(
             flops=3_000_000_000, bytes_accessed=12_000_000, transcendentals=3_000_000
@@ -451,6 +451,13 @@
         column_map.reshape(1, LANES),
         batch_count.reshape(1, 32),
     )
+    return pl.pallas_call(
+        hand_on,
+        out_shape=tuple(jax.ShapeDtypeStruct(r.shape, r.dtype) for r in results),
+        in_specs=[vmem] * 3,
+        out_specs=(vmem,) * 3,
+        compiler_params=pltpu.CompilerParams(vmem_limit_bytes=VMEM_BYTES),
+    )(*results)
 
 
 def solution(mesh):

time: 48.1 us -> 44.7 us (0.929)
  local copies, waits for them, and re-layouts: 4.34 us -> 0 us
  Pallas kernels: 42.9 us -> 43.9 us
    unnamed x3 -> x0, local copies, waits for them, and re-layouts: 4.34 us -> none
    pallas_call x0 -> x1, Pallas kernels: none -> 1.59 us  [body(): pl.pallas_call(hand_on, out_shape=tuple((jax.ShapeDtypeStruct(r.shape, r....]
    pallas_call x1, Pallas kernels: 42.9 us -> 42.3 us  [body(): pl.pallas_call(kernel, out_shape=(jax.ShapeDtypeStruct((4, 32, LANES), f3...]
where the time goes in v4:
time: 44.7 us; the launch traced here: 44.6 us
  Pallas kernels  43.9 us (98%)
  between operations  0.64 us (1%)
    pallas_call x1, Pallas kernels, body(): pl.pallas_call(kernel, out_shape=(jax.ShapeDtypeStruct((4, 32, LANES), f3...  42.3 us
    pallas_call x1, Pallas kernels, body(): pl.pallas_call(hand_on, out_shape=tuple((jax.ShapeDtypeStruct(r.shape, r....  1.59 us

profile of v4, /device:TPU:1, one launch (start us, length us, event | category | flops | bytes accessed | tf_op | source)
XLA Modules:
  0.0 44.6 jit_solution(6877346439120437864)
XLA Ops:
  0.6 42.3 %shard_map.103 = (f32[4,32,128]{2,1,0:T(8,128)}, f32[16,2048]{1,0:T(8,128)}, f32[16,128]{1,0:T(8,128)}) custom-call(f32[4,32,128]{2,1,0:T(8,128)} %field.1, f32[4,32,128]{2,1,0:T(8,128)} %wind.1, bf16[128,2048]{1,0:T(8,128)(2,1)} %w_in.1, bf16[2048,2048]{1,0:T(8,128)(2,1)} %w_mid.1, bf16[2048,128]{1,0:T(8,128)(2,1)} %w_out.1, f32[128,128]{1,0:T(8,128)} %targets.1, ...), custom_call_target="tpu_custom_call" | custom-call | flops 3000000000 | bytes 12000000 | tf_op jit(solution)/shard_map/pallas_call | solution.py:386
  43.0 1.6 %shard_map.104 = (f32[4,32,128]{2,1,0:T(8,128)}, f32[16,2048]{1,0:T(8,128)}, f32[16,128]{1,0:T(8,128)}) custom-call(f32[4,32,128]{2,1,0:T(8,128)} %get-tuple-element.6.a, f32[16,2048]{1,0:T(8,128)} %get-tuple-element.7.b, f32[16,128]{1,0:T(8,128)} %get-tuple-element.8.c), custom_call_target="tpu_custom_call" | custom-call | tf_op jit(solution)/shard_map/pallas_call | solution.py:454

commit v5 on v4

--- a/solution.py
+++ b/solution.py
@@ -33,9 +33,9 @@
     field_out, grad_mid, grad_out,
     cmap, batch, ext, gust, mids, win, wint, wout, goal, first, firsts, second, slope, inputs,
     step, outgoing, mine, cnt_out, cnt_in, sum_out, sum_in,
-    part, got_one, half, got_h,
+    part, got_one, half_0, half_1, got_0, got_1,
     load_sem, mid_sem, halo_s, halo_r, in_s, in_r, cnt_s, cnt_r, sum_s, sum_r,
-    m_s, m_r, one_s, one_r, two_s, two_r,
+    m_s, m_r, one_s, one_r, two_s, two_r, passed,
 ):
     grp, lon = lax.axis_index("grp"), lax.axis_index("lon")
     place, zh = lax.div(lon, 2), lax.rem(lon, 2)
@@ -82,9 +82,8 @@
         return pltpu.make_async_copy(w_mid.at[:, c * WIDE : c * WIDE + WIDE], mids.at[c], mid_sem.at[c])
 
     barrier = pltpu.get_barrier_semaphore()
-    far = 2 * zh - 1
-    greeted = [beside(dg, far) for dg in (-1, 0, 1)]
-    greeted += [plane(k) for k in range(1, SIDE * SIDE)] + [ring(k) for k in range(1, RANKS)]
+    x_peers, y_peers = [along_x(k) for k in range(1, SIDE)], [along_y(k) for k in range(1, SIDE)]
+    greeted = [ring(k) for k in range(1, RANKS)] + x_peers + y_peers
     for other in greeted:
         pl.semaphore_signal(barrier, inc=1, device_id=other, device_id_type=MESH)
 
@@ -135,7 +134,11 @@
         remote(src, dst, halo_s.at[i], halo_r.at[i], beside(dg, dl))
         for i, (src, dst, dg, dl) in enumerate(halo)
     ]
-    for copy in halo_copies + cnt_copies + in_copies:
+    for copy in cnt_copies:
+        copy.start()
+    for other in x_peers + y_peers:
+        pl.semaphore_signal(passed.at[0], inc=1, device_id=other, device_id_type=MESH)
+    for copy in in_copies:
         copy.start()
 
     loads[1].wait()
@@ -156,7 +159,14 @@
         slope[:, at] = sig * (1.0 + pre * (1.0 - sig))
         return jnp.dot(act, wout[at, :], preferred_element_type=f32)
 
-    predicted = second_step(0) + second_step(1)
+    pl.semaphore_wait(passed.at[0], len(x_peers) + len(y_peers))
+    for other in x_peers:
+        pl.semaphore_signal(passed.at[1], inc=1, device_id=other, device_id_type=MESH)
+    predicted = second_step(0)
+    pl.semaphore_wait(passed.at[1], len(x_peers))
+    for copy in halo_copies:
+        copy.start()
+    predicted = predicted + second_step(1)
 
     total = cnt_out[...]
     for k in range(1, RANKS):
@@ -267,38 +277,40 @@
         both = got_one.at[q, axis, k]
         return remote(both, both, one_s.at[q, axis, k], one_r.at[q, axis, k], along_x(k))
 
-    def out_copy(q, axis, k, g, z):
+    halves, gots = (half_0, half_1), (got_0, got_1)
+
+    def out_copy(n, axis, k, g, z):
         if axis == 0:
             at = lax.rem(y + k, SIDE)
             lon_at = x * (2 * SIDE) + at * 2 + z
         else:
             at = lax.rem(x + k, SIDE)
             lon_at = at * (2 * SIDE) + y * 2 + z
-        src, dst = half.at[q, axis, at, g, z], got_h.at[q, k * RANKS + rank]
-        return remote(src, dst, two_s.at[q], two_r.at[q], (2 * axis + g, lon_at))
-
-    def own_copy(q, axis, g, z):
-        src = half.at[q, axis, y if axis == 0 else x, g, z]
-        return pltpu.make_async_copy(src, got_h.at[q, rank], two_r.at[q])
-
-    def send_out(q, axis):
+        src, dst = halves[n].at[axis, at, g, z], gots[n].at[k * RANKS + rank]
+        return remote(src, dst, two_s.at[n], two_r.at[n], (2 * axis + g, lon_at))
+
+    def own_copy(n, axis, g, z):
+        src = halves[n].at[axis, y if axis == 0 else x, g, z]
+        return pltpu.make_async_copy(src, gots[n].at[rank], two_r.at[n])
+
+    def send_out(n, axis):
         rows = [(g, z) for g in range(2) for z in range(2)]
         for k in (2, 1, 3):
             for g, z in rows:
-                out_copy(q, axis, k, g, z).start()
+                out_copy(n, axis, k, g, z).start()
         for g, z in rows:
             here = (grp == 2 * axis + g) & (zh == z)
 
             @pl.when(here)
             def _():
-                own_copy(q, axis, g, z).start()
+                own_copy(n, axis, g, z).start()
 
             @pl.when(jnp.logical_not(here))
             def _():
-                out_copy(q, axis, 0, g, z).start()
-
-    def out_all(q):
-        return remote(got_h.at[q], got_h.at[q], two_s.at[q], two_r.at[q], ring(1))
+                out_copy(n, axis, 0, g, z).start()
+
+    def out_all(n):
+        return remote(gots[n], gots[n], two_s.at[n], two_r.at[n], ring(1))
 
     def make_part(q, product):
         for g in (0, 2, 1, 3):
@@ -306,17 +318,18 @@
             for k in (2, 1, 3):
                 one_copy(q, k, g).start()
 
-    def reduce_one(q):
+    def reduce_one(n, parts):
         for axis in range(2):
-            total = part[q, 0:2, x] if axis == 0 else part[q, 2:4, :, y]
-            total = total.astype(f32)
-            for k in range(1, SIDE):
-                one_pair(q, axis, k).wait_recv()
-                total = total + got_one[q, axis, k].astype(f32)
-            total = total.astype(bf16).reshape(2, SIDE, 2, 16, LANES)
-            for g in range(2):
-                half[q, axis, :, g] = total[g]
-            send_out(q, axis)
+            for i, q in enumerate(parts):
+                total = part[q, 0:2, x] if axis == 0 else part[q, 2:4, :, y]
+                total = total.astype(f32)
+                for k in range(1, SIDE):
+                    one_pair(q, axis, k).wait_recv()
+                    total = total + got_one[q, axis, k].astype(f32)
+                total = total.astype(bf16).reshape(2, SIDE, 2, 16, LANES)
+                for g in range(2):
+                    halves[n][axis, :, g, :, i] = total[g]
+            send_out(n, axis)
 
     make_part(
         0,
@@ -347,15 +360,14 @@
                 firsts[g * 512 : g * 512 + 512, :], mine[h], preferred_element_type=f32
             ),
         )
-    for q in range(3):
-        reduce_one(q)
+    reduce_one(0, (0,))
+    reduce_one(1, (1, 2))
 
     out_all(0).wait_recv()
-    grad_out[...] = jnp.sum(got_h[0].astype(f32), 0)
+    grad_out[...] = jnp.sum(got_0[:, 0].astype(f32), 0)
+    out_all(1).wait_recv()
     for h in range(2):
-        out_all(1 + h).wait_recv()
-        got = got_h[1 + h].astype(f32).reshape(SIDE, RANKS, 16, LANES)
-        total = jnp.sum(got, 0)
+        total = jnp.sum(got_1[:, h].astype(f32).reshape(SIDE, RANKS, 16, LANES), 0)
         for t in range(RANKS):
             at = t * BLOCK + h * LANES
             grad_mid[:, at : at + LANES] = total[t]
@@ -369,8 +381,9 @@
         for k in range(1, SIDE):
             for axis in range(2):
                 one_pair(q, axis, k).wait_send()
-        sent = got_h.at[q, 1:]
-        remote(sent, sent, two_s.at[q], two_r.at[q], ring(1)).wait_send()
+    for n in range(2):
+        sent = gots[n].at[1:]
+        remote(sent, sent, two_s.at[n], two_r.at[n], ring(1)).wait_send()
 
 
 def hand_on(a, b, c, a_out, b_out, c_out):
@@ -416,8 +429,10 @@
             V((SIDE * SIDE, 8, LANES), f32),
             V((3, 4, SIDE, SIDE, 32, LANES), bf16),
             V((3, 2, SIDE, 2, SIDE, 32, LANES), bf16),
-            V((3, 2, SIDE, 2, 2, 16, LANES), bf16),
-            V((3, SIDE * RANKS, 16, LANES), bf16),
+            V((2, SIDE, 2, 2, 1, 16, LANES), bf16),
+            V((2, SIDE, 2, 2, 2, 16, LANES), bf16),
+            V((SIDE * RANKS, 1, 16, LANES), bf16),
+            V((SIDE * RANKS, 2, 16, LANES), bf16),
             dma((7,)),
             dma((4,)),
             dma((12,)),
@@ -432,8 +447,9 @@
             dma((2, RANKS)),
             dma((3, 2, SIDE)),
             dma((3, 2, SIDE)),
-            dma((3,)),
-            dma((3,)),
+            dma((2,)),
+            dma((2,)),
+            pltpu.SemaphoreType.REGULAR((2,)),
         ],
         compiler_params=pltpu.CompilerParams(
             collective_id=0, has_side_effects=True, vmem_limit_bytes=VMEM_BYTES

time: 44.7 us -> 42 us (0.940)
  Pallas kernels: 43.9 us -> 41.3 us
    pallas_call x1, Pallas kernels: 42.3 us -> 39.7 us  [body(): pl.pallas_call(kernel, out_shape=(jax.ShapeDtypeStruct((4, 32, LANES), f3...]
where the time goes in v5:
time: 42 us; the launch traced here: 41.9 us
  Pallas kernels  41.3 us (98%)
  between operations  0.64 us (2%)
    pallas_call x1, Pallas kernels, body(): pl.pallas_call(kernel, out_shape=(jax.ShapeDtypeStruct((4, 32, LANES), f3...  39.7 us
    pallas_call x1, Pallas kernels, body(): pl.pallas_call(hand_on, out_shape=tuple((jax.ShapeDtypeStruct(r.shape, r....  1.59 us

profile of v5, /device:TPU:1, one launch (start us, length us, event | category | flops | bytes accessed | tf_op | source)
XLA Modules:
  0.0 41.9 jit_solution(6283968565517930715)
XLA Ops:
  0.6 39.7 %shard_map.103 = (f32[4,32,128]{2,1,0:T(8,128)}, f32[16,2048]{1,0:T(8,128)}, f32[16,128]{1,0:T(8,128)}) custom-call(f32[4,32,128]{2,1,0:T(8,128)} %field.1, f32[4,32,128]{2,1,0:T(8,128)} %wind.1, bf16[128,2048]{1,0:T(8,128)(2,1)} %w_in.1, bf16[2048,2048]{1,0:T(8,128)(2,1)} %w_mid.1, bf16[2048,128]{1,0:T(8,128)(2,1)} %w_out.1, f32[128,128]{1,0:T(8,128)} %targets.1, ...), custom_call_target="tpu_custom_call" | custom-call | flops 3000000000 | bytes 12000000 | tf_op jit(solution)/shard_map/pallas_call | solution.py:399
  40.3 1.6 %shard_map.104 = (f32[4,32,128]{2,1,0:T(8,128)}, f32[16,2048]{1,0:T(8,128)}, f32[16,128]{1,0:T(8,128)}) custom-call(f32[4,32,128]{2,1,0:T(8,128)} %get-tuple-element.6.a, f32[16,2048]{1,0:T(8,128)} %get-tuple-element.7.b, f32[16,128]{1,0:T(8,128)} %get-tuple-element.8.c), custom_call_target="tpu_custom_call" | custom-call | tf_op jit(solution)/shard_map/pallas_call | solution.py:470

commit v6 on v5

--- a/solution.py
+++ b/solution.py
@@ -31,7 +31,7 @@
 def kernel(
     field, wind, w_in, w_mid, w_out, targets, cmap_in, batch_in,
     field_out, grad_mid, grad_out,
-    cmap, batch, ext, gust, mids, win, wint, wout, goal, first, firsts, second, slope, inputs,
+    cmap, batch, ext, mids, win, wint, wout, goal, first, firsts, second, slope, inputs,
     step, outgoing, mine, cnt_out, cnt_in, sum_out, sum_in,
     part, got_one, half_0, half_1, got_0, got_1,
     load_sem, mid_sem, halo_s, halo_r, in_s, in_r, cnt_s, cnt_r, sum_s, sum_r,
@@ -69,9 +69,9 @@
         )
 
     loads = [
-        pltpu.make_async_copy(field, ext.at[2:6, 8:40], load_sem.at[0]),
+        pltpu.make_async_copy(field, ext.at[0, 2:6, 8:40], load_sem.at[0]),
         pltpu.make_async_copy(w_in, win, load_sem.at[1]),
-        pltpu.make_async_copy(wind, gust.at[1:5, 8:40], load_sem.at[2]),
+        pltpu.make_async_copy(wind, ext.at[1, 2:6, 8:40], load_sem.at[2]),
         pltpu.make_async_copy(w_out, wout, load_sem.at[3]),
         pltpu.make_async_copy(targets, goal, load_sem.at[4]),
         pltpu.make_async_copy(cmap_in, cmap, load_sem.at[5]),
@@ -82,16 +82,17 @@
         return pltpu.make_async_copy(w_mid.at[:, c * WIDE : c * WIDE + WIDE], mids.at[c], mid_sem.at[c])
 
     barrier = pltpu.get_barrier_semaphore()
+    far = 2 * zh - 1
     x_peers, y_peers = [along_x(k) for k in range(1, SIDE)], [along_y(k) for k in range(1, SIDE)]
     greeted = [ring(k) for k in range(1, RANKS)] + x_peers + y_peers
     for other in greeted:
         pl.semaphore_signal(barrier, inc=1, device_id=other, device_id_type=MESH)
 
-    for i in (0, 2, 5, 1):
+    for i in (0, 2, 5, 1, 3):
         loads[i].start()
     for c in range(4):
         mid_load(c).start()
-    for i in (3, 4, 6):
+    for i in (4, 6):
         loads[i].start()
 
     loads[5].wait()
@@ -102,7 +103,7 @@
     cnt_out[...] = jnp.broadcast_to(own_count, (8, LANES))
 
     loads[0].wait()
-    own_in = ext[2:6, 8:40].reshape(LANES, LANES).astype(bf16)
+    own_in = ext[0, 2:6, 8:40].reshape(LANES, LANES).astype(bf16)
     inputs[wide(rank, LANES), :] = own_in
     loads[2].wait()
     pl.semaphore_wait(barrier, len(greeted))
@@ -116,20 +117,22 @@
     cnt_copies = [
         remote(cnt_out, cnt_in.at[k], cnt_s.at[k], cnt_r.at[k], ring(k)) for k in range(1, RANKS)
     ]
+    def edge(dl):
+        return pl.ds(pl.multiple_of(20 + 12 * dl, 8), 8)
+
+    def rim(dl):
+        return pl.ds(pl.multiple_of(20 - 20 * dl, 8), 8)
+
     halo = [
-        (ext.at[2:4, 8:40], ext.at[6:8, 8:40], -1, 0),
-        (ext.at[4:6, 8:40], ext.at[0:2, 8:40], 1, 0),
-        (ext.at[2:6, 8:16], ext.at[2:6, 40:48], 0, -1),
-        (ext.at[2:6, 32:40], ext.at[2:6, 0:8], 0, 1),
-        (ext.at[2:3, 8:16], ext.at[6:7, 40:48], -1, -1),
-        (ext.at[2:3, 32:40], ext.at[6:7, 0:8], -1, 1),
-        (ext.at[5:6, 8:16], ext.at[1:2, 40:48], 1, -1),
-        (ext.at[5:6, 32:40], ext.at[1:2, 0:8], 1, 1),
-        (gust.at[1:2, 8:40], gust.at[5:6, 8:40], -1, 0),
-        (gust.at[4:5, 8:40], gust.at[0:1, 8:40], 1, 0),
-        (gust.at[1:5, 8:16], gust.at[1:5, 40:48], 0, -1),
-        (gust.at[1:5, 32:40], gust.at[1:5, 0:8], 0, 1),
-    ]
+        (ext.at[:, 2:4, 8:40], ext.at[:, 6:8, 8:40], -1, 0),
+        (ext.at[:, 4:6, 8:40], ext.at[:, 0:2, 8:40], 1, 0),
+    ]
+    for dl in (-far, far):
+        halo += [
+            (ext.at[:, 2:6, edge(dl)], ext.at[:, 2:6, rim(dl)], 0, dl),
+            (ext.at[0, 2, edge(dl)], ext.at[0, 6, rim(dl)], -1, dl),
+            (ext.at[0, 5, edge(dl)], ext.at[0, 1, rim(dl)], 1, dl),
+        ]
     halo_copies = [
         remote(src, dst, halo_s.at[i], halo_r.at[i], beside(dg, dl))
         for i, (src, dst, dg, dl) in enumerate(halo)
@@ -138,7 +141,7 @@
         copy.start()
     for other in x_peers + y_peers:
         pl.semaphore_signal(passed.at[0], inc=1, device_id=other, device_id_type=MESH)
-    for copy in in_copies:
+    for copy in halo_copies[:5] + in_copies:
         copy.start()
 
     loads[1].wait()
@@ -164,9 +167,8 @@
         pl.semaphore_signal(passed.at[1], inc=1, device_id=other, device_id_type=MESH)
     predicted = second_step(0)
     pl.semaphore_wait(passed.at[1], len(x_peers))
-    for copy in halo_copies:
+    for copy in halo_copies[5:]:
         copy.start()
-    predicted = predicted + second_step(1)
 
     total = cnt_out[...]
     for k in range(1, RANKS):
@@ -180,7 +182,8 @@
     for copy in sum_copies:
         copy.start()
 
-    predicted = predicted + second_step(2) + second_step(3)
+    for c in range(1, 4):
+        predicted = predicted + second_step(c)
 
     def turn_step(c, carry):
         wint[wide(c, BLOCK), :] = win[:, wide(c, BLOCK)].T
@@ -204,18 +207,18 @@
 
     for row in range(-1, 5):
         i = row + 2
-        c = masked(row, ext[i, 7:41])
-        e, w = masked(row, ext[i, 8:42]), masked(row, ext[i, 6:40])
-        n, s = masked(row + 1, ext[i + 1, 7:41]), masked(row - 1, ext[i - 1, 7:41])
-        step[row + 1, 7:41] = masked(row, advanced(c, n, s, e, w, gust[row + 1, 7:41]))
+        c = masked(row, ext[0, i, 7:41])
+        e, w = masked(row, ext[0, i, 8:42]), masked(row, ext[0, i, 6:40])
+        n, s = masked(row + 1, ext[0, i + 1, 7:41]), masked(row - 1, ext[0, i - 1, 7:41])
+        step[row + 1, 7:41] = masked(row, advanced(c, n, s, e, w, ext[1, i, 7:41]))
     current = []
     for row in range(4):
         c = step[row + 1, 8:40]
         e, w = step[row + 1, 9:41], step[row + 1, 7:39]
         n, s = step[row + 2, 8:40], step[row, 8:40]
-        current.append(advanced(c, n, s, e, w, gust[row + 1, 8:40]))
+        current.append(advanced(c, n, s, e, w, ext[1, row + 2, 8:40]))
     current = jnp.concatenate(current, 0)
-    start = ext[2:6, 8:40].reshape(LANES, LANES)
+    start = ext[0, 2:6, 8:40].reshape(LANES, LANES)
     increment = (current - start).astype(bf16).astype(f32)
     loads[4].wait()
     wanted = jnp.where(is_trainer, goal[...], increment)
@@ -349,7 +352,7 @@
         firsts[wide(c, BLOCK), wide(n, 512)] = (pre * sigmoid(pre)).astype(bf16)
         return carry
 
-    lax.fori_loop(0, 2 * RANKS, firsts_step, 0)
+    lax.fori_loop(0, 2 * RANKS, firsts_step, 0, unroll=2)
 
     for h in range(2):
         for k in range(1, RANKS):
@@ -361,7 +364,16 @@
             ),
         )
     reduce_one(0, (0,))
+    for copy in in_copies + cnt_copies + halo_copies + sum_copies:
+        copy.wait_send()
+    for h in range(2):
+        for k in range(1, RANKS):
+            m_copy(k, h).wait_send()
     reduce_one(1, (1, 2))
+    for q in range(3):
+        for k in range(1, SIDE):
+            for axis in range(2):
+                one_pair(q, axis, k).wait_send()
 
     out_all(0).wait_recv()
     grad_out[...] = jnp.sum(got_0[:, 0].astype(f32), 0)
@@ -372,15 +384,6 @@
             at = t * BLOCK + h * LANES
             grad_mid[:, at : at + LANES] = total[t]
 
-    for copy in in_copies + cnt_copies + halo_copies + sum_copies:
-        copy.wait_send()
-    for h in range(2):
-        for k in range(1, RANKS):
-            m_copy(k, h).wait_send()
-    for q in range(3):
-        for k in range(1, SIDE):
-            for axis in range(2):
-                one_pair(q, axis, k).wait_send()
     for n in range(2):
         sent = gots[n].at[1:]
         remote(sent, sent, two_s.at[n], two_r.at[n], ring(1)).wait_send()
@@ -408,8 +411,7 @@
         scratch_shapes=[
             V((1, LANES), jnp.int32),
             V((1, 32), jnp.int32),
-            V((8, 48, LANES), f32),
-            V((6, 48, LANES), f32),
+            V((2, 8, 48, LANES), f32),
             V((4, hid, WIDE), bf16),
             V((LANES, hid), bf16),
             V((hid, LANES), bf16),
@@ -435,8 +437,8 @@
             V((SIDE * RANKS, 2, 16, LANES), bf16),
             dma((7,)),
             dma((4,)),
-            dma((12,)),
-            dma((12,)),
+            dma((8,)),
+            dma((8,)),
             dma((RANKS,)),
             dma((RANKS,)),
             dma((RANKS,)),

time: 42 us -> 41.4 us (0.986)
  Pallas kernels: 41.3 us -> 40.7 us
    pallas_call x1, Pallas kernels: 39.7 us -> 39.1 us  [body(): pl.pallas_call(kernel, out_shape=(jax.ShapeDtypeStruct((4, 32, LANES), f3...]
where the time goes in v6:
time: 41.4 us; the launch traced here: 41.3 us
  Pallas kernels  40.7 us (98%)
  between operations  0.64 us (2%)
    pallas_call x1, Pallas kernels, body(): pl.pallas_call(kernel, out_shape=(jax.ShapeDtypeStruct((4, 32, LANES), f3...  39.1 us
    pallas_call x1, Pallas kernels, body(): pl.pallas_call(hand_on, out_shape=tuple((jax.ShapeDtypeStruct(r.shape, r....  1.59 us

profile of v6, /device:TPU:1, one launch (start us, length us, event | category | flops | bytes accessed | tf_op | source)
XLA Modules:
  0.0 41.3 jit_solution(12009235116990749869)
XLA Ops:
  0.6 39.1 %shard_map.103 = (f32[4,32,128]{2,1,0:T(8,128)}, f32[16,2048]{1,0:T(8,128)}, f32[16,128]{1,0:T(8,128)}) custom-call(f32[4,32,128]{2,1,0:T(8,128)} %field.1, f32[4,32,128]{2,1,0:T(8,128)} %wind.1, bf16[128,2048]{1,0:T(8,128)(2,1)} %w_in.1, bf16[2048,2048]{1,0:T(8,128)(2,1)} %w_mid.1, bf16[2048,128]{1,0:T(8,128)(2,1)} %w_out.1, f32[128,128]{1,0:T(8,128)} %targets.1, ...), custom_call_target="tpu_custom_call" | custom-call | flops 3000000000 | bytes 12000000 | tf_op jit(solution)/shard_map/pallas_call | solution.py:402
  39.7 1.6 %shard_map.104 = (f32[4,32,128]{2,1,0:T(8,128)}, f32[16,2048]{1,0:T(8,128)}, f32[16,128]{1,0:T(8,128)}) custom-call(f32[4,32,128]{2,1,0:T(8,128)} %get-tuple-element.6.a, f32[16,2048]{1,0:T(8,128)} %get-tuple-element.7.b, f32[16,128]{1,0:T(8,128)} %get-tuple-element.8.c), custom_call_target="tpu_custom_call" | custom-call | tf_op jit(solution)/shard_map/pallas_call | solution.py:472

commit v7 on v6

--- a/solution.py
+++ b/solution.py
@@ -88,7 +88,7 @@
     for other in greeted:
         pl.semaphore_signal(barrier, inc=1, device_id=other, device_id_type=MESH)
 
-    for i in (0, 2, 5, 1, 3):
+    for i in (5, 0, 2, 1, 3):
         loads[i].start()
     for c in range(4):
         mid_load(c).start()
@@ -102,10 +102,6 @@
     own_count = jnp.sum(match, 0, keepdims=True) * jnp.where(is_trainer, 0.0, 1.0)
     cnt_out[...] = jnp.broadcast_to(own_count, (8, LANES))
 
-    loads[0].wait()
-    own_in = ext[0, 2:6, 8:40].reshape(LANES, LANES).astype(bf16)
-    inputs[wide(rank, LANES), :] = own_in
-    loads[2].wait()
     pl.semaphore_wait(barrier, len(greeted))
 
     in_copies = [
@@ -141,8 +137,16 @@
         copy.start()
     for other in x_peers + y_peers:
         pl.semaphore_signal(passed.at[0], inc=1, device_id=other, device_id_type=MESH)
+    loads[0].wait()
+    own_in = ext[0, 2:6, 8:40].reshape(LANES, LANES).astype(bf16)
+    inputs[wide(rank, LANES), :] = own_in
+    loads[2].wait()
     for copy in halo_copies[:5] + in_copies:
         copy.start()
+
+    pl.semaphore_wait(passed.at[0], len(x_peers) + len(y_peers))
+    for other in x_peers:
+        pl.semaphore_signal(passed.at[1], inc=1, device_id=other, device_id_type=MESH)
 
     loads[1].wait()
     own_in = inputs[wide(rank, LANES), :]
@@ -162,9 +166,6 @@
         slope[:, at] = sig * (1.0 + pre * (1.0 - sig))
         return jnp.dot(act, wout[at, :], preferred_element_type=f32)
 
-    pl.semaphore_wait(passed.at[0], len(x_peers) + len(y_peers))
-    for other in x_peers:
-        pl.semaphore_signal(passed.at[1], inc=1, device_id=other, device_id_type=MESH)
     predicted = second_step(0)
     pl.semaphore_wait(passed.at[1], len(x_peers))
     for copy in halo_copies[5:]:

time: 41.4 us -> 41.4 us (level)
  no operation moved by 1% of the time
where the time goes in v7:
time: 41.4 us; the launch traced here: 41.3 us
  Pallas kernels  40.7 us (98%)
  between operations  0.64 us (2%)
    pallas_call x1, Pallas kernels, body(): pl.pallas_call(kernel, out_shape=(jax.ShapeDtypeStruct((4, 32, LANES), f3...  39.1 us
    pallas_call x1, Pallas kernels, body(): pl.pallas_call(hand_on, out_shape=tuple((jax.ShapeDtypeStruct(r.shape, r....  1.59 us

profile of v7, /device:TPU:1, one launch (start us, length us, event | category | flops | bytes accessed | tf_op | source)
XLA Modules:
  0.0 41.3 jit_solution(3376627297235749928)
XLA Ops:
  0.6 39.1 %shard_map.103 = (f32[4,32,128]{2,1,0:T(8,128)}, f32[16,2048]{1,0:T(8,128)}, f32[16,128]{1,0:T(8,128)}) custom-call(f32[4,32,128]{2,1,0:T(8,128)} %field.1, f32[4,32,128]{2,1,0:T(8,128)} %wind.1, bf16[128,2048]{1,0:T(8,128)(2,1)} %w_in.1, bf16[2048,2048]{1,0:T(8,128)(2,1)} %w_mid.1, bf16[2048,128]{1,0:T(8,128)(2,1)} %w_out.1, f32[128,128]{1,0:T(8,128)} %targets.1, ...), custom_call_target="tpu_custom_call" | custom-call | flops 3000000000 | bytes 12000000 | tf_op jit(solution)/shard_map/pallas_call | solution.py:403
  39.7 1.6 %shard_map.104 = (f32[4,32,128]{2,1,0:T(8,128)}, f32[16,2048]{1,0:T(8,128)}, f32[16,128]{1,0:T(8,128)}) custom-call(f32[4,32,128]{2,1,0:T(8,128)} %get-tuple-element.6.a, f32[16,2048]{1,0:T(8,128)} %get-tuple-element.7.b, f32[16,128]{1,0:T(8,128)} %get-tuple-element.8.c), custom_call_target="tpu_custom_call" | custom-call | tf_op jit(solution)/shard_map/pallas_call | solution.py:473

commit v8 on v6

--- a/solution.py
+++ b/solution.py
@@ -33,7 +33,7 @@
     field_out, grad_mid, grad_out,
     cmap, batch, ext, mids, win, wint, wout, goal, first, firsts, second, slope, inputs,
     step, outgoing, mine, cnt_out, cnt_in, sum_out, sum_in,
-    part, got_one, half_0, half_1, got_0, got_1,
+    part, got_one, half, got,
     load_sem, mid_sem, halo_s, halo_r, in_s, in_r, cnt_s, cnt_r, sum_s, sum_r,
     m_s, m_r, one_s, one_r, two_s, two_r, passed,
 ):
@@ -280,7 +280,8 @@
         both = got_one.at[q, axis, k]
         return remote(both, both, one_s.at[q, axis, k], one_r.at[q, axis, k], along_x(k))
 
-    halves, gots = (half_0, half_1), (got_0, got_1)
+    halves = [half.at[q] for q in range(3)]
+    gots = [got.at[q] for q in range(3)]
 
     def out_copy(n, axis, k, g, z):
         if axis == 0:
@@ -331,7 +332,7 @@
                     total = total + got_one[q, axis, k].astype(f32)
                 total = total.astype(bf16).reshape(2, SIDE, 2, 16, LANES)
                 for g in range(2):
-                    halves[n][axis, :, g, :, i] = total[g]
+                    half[n, axis, :, g, :, i] = total[g]
             send_out(n, axis)
 
     make_part(
@@ -369,22 +370,23 @@
     for h in range(2):
         for k in range(1, RANKS):
             m_copy(k, h).wait_send()
-    reduce_one(1, (1, 2))
+    reduce_one(1, (1,))
+    reduce_one(2, (2,))
     for q in range(3):
         for k in range(1, SIDE):
             for axis in range(2):
                 one_pair(q, axis, k).wait_send()
 
     out_all(0).wait_recv()
-    grad_out[...] = jnp.sum(got_0[:, 0].astype(f32), 0)
-    out_all(1).wait_recv()
+    grad_out[...] = jnp.sum(got[0, :, 0].astype(f32), 0)
     for h in range(2):
-        total = jnp.sum(got_1[:, h].astype(f32).reshape(SIDE, RANKS, 16, LANES), 0)
+        out_all(1 + h).wait_recv()
+        total = jnp.sum(got[1 + h, :, 0].astype(f32).reshape(SIDE, RANKS, 16, LANES), 0)
         for t in range(RANKS):
             at = t * BLOCK + h * LANES
             grad_mid[:, at : at + LANES] = total[t]
 
-    for n in range(2):
+    for n in range(3):
         sent = gots[n].at[1:]
         remote(sent, sent, two_s.at[n], two_r.at[n], ring(1)).wait_send()
 
@@ -431,10 +433,8 @@
             V((SIDE * SIDE, 8, LANES), f32),
             V((3, 4, SIDE, SIDE, 32, LANES), bf16),
             V((3, 2, SIDE, 2, SIDE, 32, LANES), bf16),
-            V((2, SIDE, 2, 2, 1, 16, LANES), bf16),
-            V((2, SIDE, 2, 2, 2, 16, LANES), bf16),
-            V((SIDE * RANKS, 1, 16, LANES), bf16),
-            V((SIDE * RANKS, 2, 16, LANES), bf16),
+            V((3, 2, SIDE, 2, 2, 1, 16, LANES), bf16),
+            V((3, SIDE * RANKS, 1, 16, LANES), bf16),
             dma((7,)),
             dma((4,)),
             dma((8,)),
@@ -449,8 +449,8 @@
             dma((2, RANKS)),
             dma((3, 2, SIDE)),
             dma((3, 2, SIDE)),
-            dma((2,)),
-            dma((2,)),
+            dma((3,)),
+            dma((3,)),
             pltpu.SemaphoreType.REGULAR((2,)),
         ],
         compiler_params=pltpu.CompilerParams(

time: 41.4 us -> 41.4 us (level)
  no operation moved by 1% of the time
where the time goes in v8:
time: 41.4 us; the launch traced here: 41.2 us
  Pallas kernels  40.6 us (98%)
  between operations  0.64 us (2%)
    pallas_call x1, Pallas kernels, body(): pl.pallas_call(kernel, out_shape=(jax.ShapeDtypeStruct((4, 32, LANES), f3...  39 us
    pallas_call x1, Pallas kernels, body(): pl.pallas_call(hand_on, out_shape=tuple((jax.ShapeDtypeStruct(r.shape, r....  1.59 us

profile of v8, /device:TPU:1, one launch (start us, length us, event | category | flops | bytes accessed | tf_op | source)
XLA Modules:
  0.0 41.2 jit_solution(15194844665782743942)
XLA Ops:
  0.6 39.0 %shard_map.103 = (f32[4,32,128]{2,1,0:T(8,128)}, f32[16,2048]{1,0:T(8,128)}, f32[16,128]{1,0:T(8,128)}) custom-call(f32[4,32,128]{2,1,0:T(8,128)} %field.1, f32[4,32,128]{2,1,0:T(8,128)} %wind.1, bf16[128,2048]{1,0:T(8,128)(2,1)} %w_in.1, bf16[2048,2048]{1,0:T(8,128)(2,1)} %w_mid.1, bf16[2048,128]{1,0:T(8,128)(2,1)} %w_out.1, f32[128,128]{1,0:T(8,128)} %targets.1, ...), custom_call_target="tpu_custom_call" | custom-call | flops 3000000000 | bytes 12000000 | tf_op jit(solution)/shard_map/pallas_call | solution.py:404
  39.7 1.6 %shard_map.104 = (f32[4,32,128]{2,1,0:T(8,128)}, f32[16,2048]{1,0:T(8,128)}, f32[16,128]{1,0:T(8,128)}) custom-call(f32[4,32,128]{2,1,0:T(8,128)} %get-tuple-element.6.a, f32[16,2048]{1,0:T(8,128)} %get-tuple-element.7.b, f32[16,128]{1,0:T(8,128)} %get-tuple-element.8.c), custom_call_target="tpu_custom_call" | custom-call | tf_op jit(solution)/shard_map/pallas_call | solution.py:472
